TPU v7x, 256 devices: a whole 4x4x8 slice. The times are simulated.
256 devices in a mesh: dp: 64 (over z, y, core), tensor: 4 (over x).
Axes of the slice: x: 4, y: 4, z: 8, core: 2. Of those that a mesh axis runs over, the one named last changes fastest.
Arguments:
- inputs: bfloat16 [8192, 8192], P('dp', 'tensor'), may hold values from -6 to 6
- cotangent: bfloat16 [8192, 1024], P('dp', 'tensor'), may hold values from -6 to 6
- frozen_key_weight: bfloat16 [8192, 1024], P(None, 'tensor'), may hold values from -0.1875 to 0.1875
- adapter_down_weight: bfloat16 [64, 16, 8192], P('dp', None, 'tensor'), may hold values from -0.0625 to 0.0625
- adapter_up_weight: bfloat16 [64, 16, 1024], P('dp', None, 'tensor'), may hold values from -0.1875 to 0.1875
- tenant_per_block: int32 [64], P('dp'), may hold values from 0 to 63
Outputs:
- grad_inputs: bfloat16 [8192, 8192], P('dp', 'tensor')
- grad_down: float32 [64, 16, 8192], P('dp', None, 'tensor')
- grad_up: float32 [64, 16, 1024], P('dp', None, 'tensor')
All inputs are finite; a program needn't handle non-finite values.
Results may differ from a plain program's by a relative error of at most 0.0034.
Values may be sent and summed in bfloat16 or wider, within the bound.
A program may use at most 128 MiB of HBM per device.

v0:
```python
import jax
import jax.numpy as jnp
from jax import lax
from jax.sharding import PartitionSpec as P

ADAPTER_SCALE = 2.0


def on_device(
    inputs, cotangent, frozen_key_weight, adapter_down_weight, adapter_up_weight, tenant_per_block
):
    token_row_count, width_portion = inputs.shape
    key_portion = cotangent.shape[1]
    block_count = tenant_per_block.shape[0]
    block_rows = token_row_count // block_count
    adapter_rank_size = adapter_down_weight.shape[1]
    held_block_count = adapter_down_weight.shape[0]
    owner_count = lax.axis_size("dp")
    tenant_number = owner_count * held_block_count
    pieces = (
        lax.all_gather(adapter_down_weight, "dp", axis=0, tiled=True),
        lax.all_gather(adapter_up_weight, "dp", axis=0, tiled=True),
    )
    piece_count = pieces[0].shape[0]
    tenant_ids = jnp.arange(piece_count, dtype=jnp.int32)
    member = (tenant_per_block[:, None] == tenant_ids[None, :]).astype(jnp.bfloat16)
    down_sum = jnp.einsum("bk,krd->brd", member, pieces[0], preferred_element_type=jnp.float32)
    up_sum = jnp.einsum("bk,krd->brd", member, pieces[1], preferred_element_type=jnp.float32)
    sel_down = down_sum
    sel_up = up_sum
    sel_down = sel_down.astype(jnp.bfloat16)
    sel_up = sel_up.astype(jnp.bfloat16)
    input_blocks = inputs.reshape(block_count, block_rows, width_portion)
    cotangent_blocks = cotangent.reshape(block_count, block_rows, key_portion)
    low_in = jnp.einsum("bnd,brd->bnr", input_blocks, sel_down, preferred_element_type=jnp.float32)
    reduced_output = ADAPTER_SCALE * jnp.einsum(
        "bnk,brk->bnr", cotangent_blocks, sel_up, preferred_element_type=jnp.float32
    )
    low_in, reduced_output = lax.psum((low_in, reduced_output), "tensor")
    reduced_input_batch = low_in.astype(jnp.bfloat16)
    low_out_b = reduced_output.astype(jnp.bfloat16)
    adapter_grad = jnp.einsum(
        "bnr,brd->bnd", low_out_b, sel_down, preferred_element_type=jnp.float32
    )
    adapter_grad = adapter_grad.reshape(token_row_count, width_portion)
    partial_grad = lax.dot_general(
        cotangent, frozen_key_weight, (((1,), (1,)), ((), ())), preferred_element_type=jnp.float32
    )
    base_grad = lax.psum_scatter(partial_grad, "tensor", scatter_dimension=1, tiled=True)
    grad_inputs = (base_grad + adapter_grad).astype(jnp.bfloat16)
    all_tenants = jnp.arange(tenant_number, dtype=jnp.int32)
    member = tenant_per_block[:, None] == all_tenants[None, :]
    member_b = member.astype(jnp.bfloat16)
    weighted_out = (member_b[:, None, :, None] * low_out_b[:, :, None, :]).reshape(
        token_row_count, tenant_number * adapter_rank_size
    )
    weighted_in = (member_b[:, None, :, None] * reduced_input_batch[:, :, None, :]).reshape(
        token_row_count, tenant_number * adapter_rank_size
    )
    down_contribution = lax.dot_general(
        weighted_out, inputs, (((0,), (0,)), ((), ())), preferred_element_type=jnp.float32
    )
    up_contribution = ADAPTER_SCALE * lax.dot_general(
        weighted_in, cotangent, (((0,), (0,)), ((), ())), preferred_element_type=jnp.float32
    )
    down_contribution = down_contribution.reshape(tenant_number, adapter_rank_size, width_portion)
    up_contribution = up_contribution.reshape(tenant_number, adapter_rank_size, key_portion)
    combined = jnp.concatenate([down_contribution, up_contribution], axis=2)
    owned = lax.psum_scatter(combined, "dp", scatter_dimension=0, tiled=True)
    grad_down = owned[:, :, :width_portion]
    grad_up = owned[:, :, width_portion:]
    return (grad_inputs, grad_down, grad_up)


def solution(mesh):
    in_specs = (
        P("dp", "tensor"),
        P("dp", "tensor"),
        P(None, "tensor"),
        P("dp", None, "tensor"),
        P("dp", None, "tensor"),
        P("dp"),
    )
    out_specs = (P("dp", "tensor"), P("dp", None, "tensor"), P("dp", None, "tensor"))
    return jax.shard_map(
        on_device, mesh=mesh, in_specs=in_specs, out_specs=out_specs, check_vma=False
    )
```

profile of v0, /device:TPU:1, one launch (start us, length us, event | category | flops | bytes accessed | tf_op | source)
XLA Modules:
  0.0 344.3 jit_solution(15051737981572516454)
XLA Ops:
  8.0 0.0 copy-start
  8.0 0.0 all-gather.2.cloned.1.call-start
  8.1 0.7 all-gather.2.cloned.1.call-update
  8.7 0.0 reduce-scatter.2.cloned.1.call-start
  8.8 5.7 %fusion.14 = f32[128,8192]{1,0:T(8,128)} fusion(bf16[128,256]{1,0:T(8,128)(2,1)} %param.7, bf16[8192,256]{1,0:T(8,128)(2,1)} %param.8), kind=kOutput, calls=%fused_computation.28 | convolution fusion | flops 536870912 | bytes 8454144 | tf_op jit(solution)/shard_map/dot_general | solution.py:46
  14.5 0.0 copy-start.2
  14.5 0.0 copy-start.1
  14.5 0.0 reduce-scatter.2.cloned.1.call-update
  14.6 0.0 all-reduce.4.cloned.1.call-start
  15.3 0.1 mul.62
  15.4 0.1 mul.63
  15.4 0.0 copy-done.2
  15.5 54.9 %all_gather.6 = bf16[64,16,256]{2,1,0:T(8,128)(2,1)S(1)} all-gather(bf16[1,16,256]{2,1,0:T(8,128)(2,1)S(1)} %copy-done.2), channel_id=1, replica_groups=mesh['dp'=64,'tensor'=4] {'dp'}, dimensions={0}, use_global_device_ids=true | all-gather | bytes 532480 | tf_op jit(solution)/shard_map/all_gather | solution.py:22
  70.4 0.3 fusion.6
  70.6 0.0 copy-done.1
  70.6 0.1 fusion.3
  70.8 24.5 %all-gather.2.cloned.1.call-done = bf16[64,16,2048]{2,1,0:T(8,128)(2,1)} async-done(((bf16[1,16,2048]{2,1,0:T(8,128)(2,1)}), bf16[64,16,2048]{2,1,0:T(8,128)(2,1)}) %all-gather.2.cloned.1.call-update) | async-done | bytes 4194320 | tf_op jit(solution)/shard_map/all_gather | solution.py:21
  95.3 6.7 %fusion = bf16[1,16,2048]{2,0,1:T(2,128)(2,1)S(1)} fusion(bf16[64,16,2048]{2,1,0:T(8,128)(2,1)} %all-gather.2.cloned.1.call-done, s32[]{:T(128)} %bitcast.51), kind=kOutput, calls=%fused_computation.1 | convolution fusion | flops 4194368 | bytes 4259844 | tf_op jit(solution)/shard_map/bk,krd->brd/dot_general | solution.py:27
  102.0 0.0 copy-done
  102.0 0.2 convolution_bitcast_fusion
  102.2 13.1 %all-reduce.1 = (bf16[1,128,16]{1,2,0:T(8,128)(2,1)S(1)}, bf16[1,128,16]{1,2,0:T(8,128)(2,1)S(1)}) all-reduce(f32[1,128,16]{1,2,0:T(8,128)S(1)} %fusion.3, f32[1,128,16]{1,2,0:T(8,128)S(1)} %convolution_bitcast_fusion), channel_id=1, replica_groups=mesh['dp'=64,'tensor'=4] {'tensor'}, use_global_device_ids=true, to_apply=%region_1.0 | all-reduce | flops 4096 | bytes 24576 | tf_op jit(solution)/shard_map/psum | solution.py:39
  115.3 0.2 bitcast_multiply_fusion.1
  115.5 0.3 convolution_multiply_fusion
  115.8 4.5 %fusion.4 = f32[64,16,2048]{2,1,0:T(8,128)} fusion(bf16[64,16,128]{2,1,0:T(8,128)(2,1)S(1)} %bitcast.53, bf16[128,2048]{1,0:T(8,128)(2,1)S(1)} %copy-done), kind=kOutput, calls=%fused_computation.9 | convolution fusion | flops 536870912 | bytes 9175040 | tf_op jit(solution)/shard_map/dot_general | solution.py:60
  120.4 7.9 %pad_maximum_fusion = f32[64,16,2304]{2,1,0:T(8,128)} fusion(f32[64,16,256]{2,1,0:T(8,128)S(1)} %bitcast.52, f32[64,16,2048]{2,1,0:T(8,128)} %fusion.4), kind=kLoop, calls=%fused_computation | loop fusion | flops 2359296 | bytes 18874368 | tf_op jit(solution)/shard_map/concatenate | solution.py:68
  128.3 0.0 all-reduce.4.cloned.1.call-update
  128.3 0.6 copy-done.3
  129.0 0.6 dynamic-slice
  129.6 2.3 fusion.2
  131.9 200.7 %all-reduce.4.cloned.1.call-done = f32[64,16,2304]{2,1,0:T(8,128)} async-done(((f32[64,16,2304]{2,1,0:T(8,128)}), f32[64,16,2304]{2,1,0:T(8,128)}) %all-reduce.4.cloned.1.call-update) | async-done | bytes 9437200
  332.6 2.2 constant_dynamic-slice_fusion
  334.8 2.0 constant_dynamic-slice_fusion.1
  (3 shorter events, 0.0 us)
Async XLA Ops:
  8.0 94.0 %copy-start = (bf16[128,2048]{1,0:T(8,128)(2,1)S(1)}, bf16[128,2048]{1,0:T(8,128)(2,1)}, u32[]{:S(2)}) copy-start(bf16[128,2048]{1,0:T(8,128)(2,1)} %param.6) | copy-start | bytes 1572868
  8.0 87.3 %all-gather.2.cloned.1.call-start = ((), (), s32[]{:S(2)}) async-start(), calls=%async_computation.2 | async-start | bytes 4259840 | tf_op jit(solution)/shard_map/all_gather | solution.py:21
  8.7 120.8 %reduce-scatter.2.cloned.1.call-start = ((), (), s32[]{:S(2)}) async-start(), calls=%async_computation.1 | async-start | bytes 5242880 | tf_op jit(solution)/shard_map/reduce_scatter | solution.py:49
  14.5 0.9 copy-start.2
  14.5 56.1 %copy-start.1 = (bf16[128,256]{1,0:T(8,128)(2,1)S(1)}, bf16[128,256]{1,0:T(8,128)(2,1)}, u32[]{:S(2)}) copy-start(bf16[128,256]{1,0:T(8,128)(2,1)} %param.7) | copy-start | bytes 196612
  14.6 318.1 %all-reduce.4.cloned.1.call-start = ((), (), s32[]{:S(2)}) async-start(), calls=%async_computation.3 | async-start | bytes 18874368
  128.3 0.7 copy-start.3
Sparse Core Ops, SparseCore 0:
  12.0 83.2 all-gather.1
  128.4 204.1 all-reduce.3
Sparse Core Ops, SparseCore 1:
  14.7 53.0 reduce-scatter.1
where the time goes:
time: 345 us; the launch traced here: 344 us
  waiting for transfers between devices  226 us (66%)
  blocking collectives  68 us (20%)
  matrix products  20.2 us (6%)
  between operations  16.2 us (5%)
  other arithmetic  8.11 us (2%)
  local copies, waits for them, and re-layouts  5.65 us (2%)
    unnamed x4, waiting for transfers between devices  201 us
    all_gather x1, blocking collectives, on_device(): lax.all_gather(adapter_up_weight, 'dp', axis=0, tiled=True)  54.9 us
    all_gather x1, waiting for transfers between devices, on_device(): lax.all_gather(adapter_down_weight, 'dp', axis=0, tiled=True)  24.5 us
    psum x1, blocking collectives, on_device(): low_in, reduced_output = lax.psum((low_in, reduced_output), 'tensor')  13.1 us
    concatenate x1, other arithmetic, on_device(): combined = jnp.concatenate([down_contribution, up_contribution], axis=2)  7.91 us
  transfers between devices with their start and end apart: 3, of which 2 were waited for; matrix products, arithmetic and copies ran while one was open for 8% of the time, Pallas kernels for 0%

commit v1 on v0

v1 whole, which is shorter than its diff:
```python
import jax
import jax.numpy as jnp
from jax import lax
from jax.experimental import pallas as pl
from jax.experimental.pallas import tpu as pltpu
from jax.sharding import PartitionSpec as P

MESH = pl.DeviceIdType.MESH
F32 = jnp.float32
BF16 = jnp.bfloat16
ADAPTER_SCALE = 2.0

Z, Y, CORES, X = 8, 4, 2, 4
G = Z * CORES
ROWS, WIDTH, KEYS, RANK, LANES = 128, 2048, 256, 16, 128
TABLE = G * RANK + 2 * RANK


def dot(a, b, dims=((1,), (0,))):
    return lax.dot_general(a, b, (dims, ((), ())), preferred_element_type=F32)


def kernel(
    inputs_hbm, cot_ref, weight_hbm, down_ref, up_ref, tenant_ref,
    out_hbm, grad_down_ref, grad_up_ref,
    xs, weight, partial, own, arrived, out_vm, cot_spread, pick,
    s1, r1, r2, s3, r3, r4, s5, r5, s6, r6, s7, r7,
    load_sem, store_sem, send_sem, recv_sem, xsend_sem, xrecv_sem,
):
    me, mx = lax.axis_index("dp"), lax.axis_index("tensor")
    z, y, c = lax.div(me, Y * CORES), lax.rem(lax.div(me, CORES), Y), lax.rem(me, CORES)
    g = z * CORES + c

    def group_member(i):
        h = lax.rem(g + G // 2 + (1 - 2 * lax.rem(i, 2)) * lax.div(i + 1, 2), G)
        return h, (lax.div(h, CORES) * Y + y) * CORES + lax.rem(h, CORES)

    def y_member(k):
        h = lax.rem(y + k, Y)
        return h, (z * Y + h) * CORES + c

    load_weight = pltpu.make_async_copy(weight_hbm, weight, load_sem.at[0])
    load_inputs = pltpu.make_async_copy(inputs_hbm, xs, load_sem.at[1])

    barrier = pltpu.get_barrier_semaphore()

    @pl.loop(0, G - 1)
    def _(i):
        _, device = group_member(i)
        pl.semaphore_signal(barrier, inc=1, device_id={"dp": device}, device_id_type=MESH)

    for k in (2, 1, 3):
        pl.semaphore_signal(barrier, inc=1, device_id={"dp": y_member(k)[1]}, device_id_type=MESH)
        pl.semaphore_signal(barrier, inc=1, device_id={"tensor": lax.rem(mx + k, X)}, device_id_type=MESH)

    load_weight.start()
    load_inputs.start()

    lane0 = RANK * lax.rem(g, 8)
    key = lax.broadcasted_iota(jnp.int32, (KEYS, KEYS), 0)
    column = lax.broadcasted_iota(jnp.int32, (KEYS, KEYS), 1)
    target = lax.div(key, RANK) * LANES + lax.rem(key, RANK) + lane0
    lane = lax.broadcasted_iota(jnp.int32, (RANK, LANES), 1)
    block_of_lane = lax.div(lane, RANK)
    tenant = jnp.full((RANK, LANES), tenant_ref[0], jnp.int32).astype(F32)
    tenant = jnp.where(block_of_lane == lax.rem(g + 1, 8), tenant, 0.0)
    cot = cot_ref[...]
    up = up_ref[0]
    for i in range(WIDTH // KEYS):
        spread = (column + i * KEYS == target).astype(F32).astype(BF16)
        cot_spread[:, i * KEYS : (i + 1) * KEYS] = dot(cot, spread).astype(BF16)
        up_spread = dot(up, spread)
        for q in range(2):
            tile = up_spread[:, q * LANES : (q + 1) * LANES] + tenant
            s1[2 * i + q, RANK:, :] = tile.astype(BF16)
    for q in range(G):
        s1[q, :RANK, :] = down_ref[0, :, q * LANES : (q + 1) * LANES]

    def group_exchange(step, src, dst):
        @pl.loop(0, G - 1)
        def _(i):
            h, device = group_member(i)
            pltpu.make_async_remote_copy(
                src.at[h], dst.at[g], send_sem.at[step], recv_sem.at[step],
                device_id={"dp": device}, device_id_type=MESH,
            ).start()

        pltpu.make_async_copy(src.at[g], dst.at[g], recv_sem.at[step]).start()

    def received(step, dst):
        pltpu.make_async_copy(dst, dst, recv_sem.at[step]).wait()

    load_weight.wait()
    for k in range(X):
        q = lax.rem(mx + k, X)

        @pl.loop(0, WIDTH // KEYS)
        def _(i):
            at = pl.multiple_of(q * WIDTH + i * KEYS, KEYS)
            product = dot(cot, weight[pl.ds(at, KEYS), :], ((1,), (1,)))
            columns = pl.ds(pl.multiple_of(i * KEYS, KEYS), KEYS)
            if k == 0:
                own[:, columns] = product
            else:
                partial[k - 1, :, columns] = product.astype(BF16)

    load_inputs.wait()
    pl.semaphore_wait(barrier, G - 1 + Y - 1 + X - 1)

    group_exchange(0, s1, r1)
    shares = []
    for k in (2, 1, 3):
        share = pltpu.make_async_remote_copy(
            partial.at[k - 1], arrived.at[k - 1], xsend_sem.at[k - 1], xrecv_sem.at[k - 1],
            device_id={"tensor": lax.rem(mx + k, X)}, device_id_type=MESH,
        )
        share.start()
        shares.append(share)
    received(0, r1)

    mine = r2.at[y]
    packed = [jnp.zeros((RANK, LANES), F32), jnp.zeros((RANK, LANES), F32)]
    for h in range(G):
        mine[h * RANK : (h + 1) * RANK, :] = r1[h, :RANK, :]
        tile = r1[h, RANK:, :].astype(F32)
        packed[h // 8] = jnp.where(block_of_lane == h % 8, tile, packed[h // 8])
    for q in range(2):
        mine[(G + q) * RANK : (G + q + 1) * RANK, :] = packed[q].astype(BF16)
    for k in (2, 1, 3):
        pltpu.make_async_remote_copy(
            mine, mine, send_sem.at[1], recv_sem.at[1],
            device_id={"dp": y_member(k)[1]}, device_id_type=MESH,
        ).start()

    rank_row = lax.broadcasted_iota(jnp.int32, (RANK, 1), 0)
    slot = lax.broadcasted_iota(jnp.int32, (RANK, Y * G * RANK), 1)
    for h in range(G):
        at = RANK * ((h + 1) % 8)
        t = r1[h, RANK:, at : at + 1].astype(F32).astype(jnp.int32)
        t_y, t_g = (t >> 1) & 3, (t >> 3) * 2 + (t & 1)
        wanted = (t_y * G + t_g) * RANK + rank_row
        pick[h * RANK : (h + 1) * RANK, :] = (slot == wanted).astype(F32).astype(BF16)

    def pick_of(q):
        return pick[:, q * KEYS : (q + 1) * KEYS]

    others = r2.at[pl.ds(0, Y - 1)]
    pltpu.make_async_copy(others, others, recv_sem.at[1]).wait()

    down_tiles = jnp.zeros((KEYS, LANES), F32)
    up_tiles = jnp.zeros((RANK, KEYS), F32)
    for q in range(Y):
        down_tiles += dot(pick_of(q), r2[q, : G * RANK, :])
        tiles = jnp.concatenate([r2[q, G * RANK : (G + 1) * RANK, :], r2[q, (G + 1) * RANK :, :]], axis=1)
        up_tiles += dot(tiles, pick_of(q), ((1,), (1,)))
    for h in range(G):
        s3[h, :RANK, :] = down_tiles[h * RANK : (h + 1) * RANK].astype(BF16)
        s3[h, RANK:, :] = up_tiles[:, h // 8 * LANES : (h // 8 + 1) * LANES].astype(BF16)
    group_exchange(2, s3, r3)
    received(2, r3)

    down_b = jnp.concatenate([r3[h, :RANK, :] for h in range(G)], axis=1)
    up_b = jnp.concatenate([r3[h, RANK:, :] for h in range(G)], axis=1)
    r4[mx, :RANK, :] = dot(down_b, xs[...], ((1,), (1,)))
    r4[mx, RANK:, :] = ADAPTER_SCALE * dot(up_b, cot_spread[...], ((1,), (1,)))
    for k in (2, 1, 3):
        pltpu.make_async_remote_copy(
            r4.at[mx], r4.at[mx], send_sem.at[3], recv_sem.at[3],
            device_id={"tensor": lax.rem(mx + k, X)}, device_id_type=MESH,
        ).start()
    others = r4.at[pl.ds(0, X - 1)]
    pltpu.make_async_copy(others, others, recv_sem.at[3]).wait()
    low = ((r4[0] + r4[1]) + (r4[2] + r4[3])).astype(BF16)
    low_in, low_out = low[:RANK], low[RANK:]

    for i in range(WIDTH // KEYS):
        columns = slice(i * KEYS, (i + 1) * KEYS)
        down_term = dot(low_out, xs[:, columns]).astype(BF16)
        up_term = (ADAPTER_SCALE * dot(low_in, cot_spread[:, columns])).astype(BF16)
        for q in range(2):
            s5[2 * i + q, :RANK, :] = down_term[:, q * LANES : (q + 1) * LANES]
            s5[2 * i + q, RANK:, :] = up_term[:, q * LANES : (q + 1) * LANES]
    group_exchange(4, s5, r5)
    for i in range(WIDTH // KEYS):
        columns = slice(i * KEYS, (i + 1) * KEYS)
        own[:, columns] += dot(low_out, down_b[:, columns], ((0,), (0,)))
    received(4, r5)

    down_terms = r5[:, :RANK, :].reshape(G * RANK, LANES)
    packed = []
    for q in range(2):
        total = r5[8 * q, RANK:, :].astype(F32)
        for h in range(8 * q + 1, 8 * q + 8):
            total += r5[h, RANK:, :].astype(F32)
        packed.append(total.astype(BF16))
    up_terms = jnp.concatenate(packed, axis=1)
    for q in range(Y):
        s6[q, : G * RANK, :] = dot(pick_of(q), down_terms, ((0,), (0,))).astype(BF16)
        sums = dot(up_terms, pick_of(q)).astype(BF16)
        s6[q, G * RANK : (G + 1) * RANK, :] = sums[:, :LANES]
        s6[q, (G + 1) * RANK :, :] = sums[:, LANES:]
    for k in (2, 1, 3):
        h, device = y_member(k)
        pltpu.make_async_remote_copy(
            s6.at[h], r6.at[y], send_sem.at[5], recv_sem.at[5],
            device_id={"dp": device}, device_id_type=MESH,
        ).start()
    pltpu.make_async_copy(s6.at[y], r6.at[y], recv_sem.at[5]).start()
    received(5, r6)

    for h in range(G + 2):
        rows = slice(h * RANK, (h + 1) * RANK)
        total = (r6[0, rows, :].astype(F32) + r6[1, rows, :].astype(F32)) + (
            r6[2, rows, :].astype(F32) + r6[3, rows, :].astype(F32)
        )
        if h < G:
            s7[h, :RANK, :] = total
        else:
            for owner in range(8 * (h - G), 8 * (h - G) + 8):
                s7[owner, RANK:, :] = total
    group_exchange(6, s7, r7)

    for share in shares:
        share.wait()
    for i in range(WIDTH // KEYS):
        columns = slice(i * KEYS, (i + 1) * KEYS)
        total = own[:, columns]
        for k in range(X - 1):
            total += arrived[k, :, columns].astype(F32)
        out_vm[:, columns] = total.astype(BF16)
    store_out = pltpu.make_async_copy(out_vm, out_hbm, store_sem)
    store_out.start()
    received(6, r7)

    for h in range(G):
        grad_down_ref[0, :, h * LANES : (h + 1) * LANES] = r7[h, :RANK, :]
    for q in range(2):
        total = jnp.zeros((RANK, LANES), F32)
        for h in range(8 * q, 8 * q + 8):
            moved = pltpu.roll(r7[h, RANK:, :], lax.rem(RANK * (h % 8) + LANES - lane0, LANES), 1)
            total = jnp.where(block_of_lane == h % 8, moved, total)
        grad_up_ref[0, :, q * LANES : (q + 1) * LANES] = total

    store_out.wait()
    for step, sent in ((0, s1), (2, s3), (4, s5), (6, s7)):
        peers = sent.at[pl.ds(0, G - 1)]
        pltpu.make_async_copy(peers, peers, send_sem.at[step]).wait()
    for step, sent in ((1, r2), (3, r4), (5, s6)):
        peers = sent.at[pl.ds(0, 3)]
        pltpu.make_async_copy(peers, peers, send_sem.at[step]).wait()


def on_device(inputs, cotangent, frozen_key_weight, adapter_down_weight, adapter_up_weight, tenant_per_block):
    hbm = pl.BlockSpec(memory_space=pl.ANY)
    vmem = pl.BlockSpec(memory_space=pltpu.VMEM)
    smem = pl.BlockSpec(memory_space=pltpu.SMEM)
    dma = pltpu.SemaphoreType.DMA
    return pl.pallas_call(
        kernel,
        out_shape=(
            jax.ShapeDtypeStruct((ROWS, WIDTH), BF16),
            jax.ShapeDtypeStruct((1, RANK, WIDTH), F32),
            jax.ShapeDtypeStruct((1, RANK, KEYS), F32),
        ),
        in_specs=[hbm, vmem, hbm, vmem, vmem, smem],
        out_specs=(hbm, vmem, vmem),
        scratch_shapes=[
            pltpu.VMEM((ROWS, WIDTH), BF16),
            pltpu.VMEM((X * WIDTH, KEYS), BF16),
            pltpu.VMEM((X - 1, ROWS, WIDTH), BF16),
            pltpu.VMEM((ROWS, WIDTH), F32),
            pltpu.VMEM((X - 1, ROWS, WIDTH), BF16),
            pltpu.VMEM((ROWS, WIDTH), BF16),
            pltpu.VMEM((ROWS, WIDTH), BF16),
            pltpu.VMEM((G * RANK, Y * G * RANK), BF16),
            pltpu.VMEM((G, 2 * RANK, LANES), BF16),
            pltpu.VMEM((G, 2 * RANK, LANES), BF16),
            pltpu.VMEM((Y, TABLE, LANES), BF16),
            pltpu.VMEM((G, 2 * RANK, LANES), BF16),
            pltpu.VMEM((G, 2 * RANK, LANES), BF16),
            pltpu.VMEM((X, 2 * RANK, LANES), F32),
            pltpu.VMEM((G, 2 * RANK, LANES), BF16),
            pltpu.VMEM((G, 2 * RANK, LANES), BF16),
            pltpu.VMEM((Y, TABLE, LANES), BF16),
            pltpu.VMEM((Y, TABLE, LANES), BF16),
            pltpu.VMEM((G, 2 * RANK, LANES), F32),
            pltpu.VMEM((G, 2 * RANK, LANES), F32),
            dma((2,)), dma, dma((7,)), dma((7,)), dma((X - 1,)), dma((X - 1,)),
        ],
        compiler_params=pltpu.CompilerParams(
            collective_id=0, has_side_effects=True, vmem_limit_bytes=40 << 20
        ),
    )(inputs, cotangent, frozen_key_weight, adapter_down_weight, adapter_up_weight, tenant_per_block)


def solution(mesh):
    in_specs = (
        P("dp", "tensor"),
        P("dp", "tensor"),
        P(None, "tensor"),
        P("dp", None, "tensor"),
        P("dp", None, "tensor"),
        P("dp"),
    )
    out_specs = (P("dp", "tensor"), P("dp", None, "tensor"), P("dp", None, "tensor"))
    return jax.shard_map(
        on_device, mesh=mesh, in_specs=in_specs, out_specs=out_specs, check_vma=False
    )
```

time: 345 us -> 69.1 us (0.20)
  waiting for transfers between devices: 226 us -> 0 us
  blocking collectives: 68 us -> 0 us
  Pallas kernels: 0 us -> 59.8 us
  matrix products: 20.2 us -> 0 us
  between operations: 16.2 us -> 1.3 us
  other arithmetic: 8.11 us -> 0 us
    unnamed x4 -> x0, waiting for transfers between devices: 201 us -> none
    pallas_call x0 -> x1, Pallas kernels: none -> 59.8 us  [on_device(): pl.pallas_call(kernel, out_shape=(jax.ShapeDtypeStruct((ROWS, WIDTH), BF1...]
    all_gather x1 -> x0, blocking collectives: 54.9 us -> none  [on_device(): lax.all_gather(adapter_up_weight, 'dp', axis=0, tiled=True)]
    all_gather x1 -> x0, waiting for transfers between devices: 24.5 us -> none  [on_device(): lax.all_gather(adapter_down_weight, 'dp', axis=0, tiled=True)]
    dot_general x8 -> x0, matrix products: 20.2 us -> none  [the longest x1 6.7 us: on_device(): jnp.einsum('bk,krd->brd', member, pieces[0], preferred_element_type=jnp.f...]
    psum x1 -> x0, blocking collectives: 13.1 us -> none  [on_device(): low_in, reduced_output = lax.psum((low_in, reduced_output), 'tensor')]
    concatenate x1 -> x0, other arithmetic: 7.91 us -> none  [on_device(): combined = jnp.concatenate([down_contribution, up_contribution], axis=2)]
    unnamed x9 -> x13, local copies, waits for them, and re-layouts: 1.26 us -> 7.65 us
  transfers between devices with their start and end apart: 3 -> 0, of which waited for: 2 -> 0; matrix products, arithmetic and copies ran while one was open for 8% -> 0% of each run, Pallas kernels for 0% -> 0%
where the time goes in v1:
time: 69.1 us; the launch traced here: 68.8 us
  Pallas kernels  59.8 us (87%)
  local copies, waits for them, and re-layouts  7.65 us (11%)
  between operations  1.3 us (2%)
    pallas_call x1, Pallas kernels, on_device(): pl.pallas_call(kernel, out_shape=(jax.ShapeDtypeStruct((ROWS, WIDTH), BF1...  59.8 us
    unnamed x13, local copies, waits for them, and re-layouts  7.65 us

profile of v1, /device:TPU:1, one launch (start us, length us, event | category | flops | bytes accessed | tf_op | source)
XLA Modules:
  0.0 68.8 jit_solution(6522502505493231166)
XLA Ops:
  1.3 0.0 copy-start
  1.3 2.2 %copy-done = bf16[8192,256]{1,0:T(8,128)(2,1)S(1)} copy-done((bf16[8192,256]{1,0:T(8,128)(2,1)S(1)}, bf16[8192,256]{1,0:T(8,128)(2,1)}, u32[]{:S(2)}) %copy-start) | copy-done | bytes 4194328
  3.5 0.0 copy-start.1
  3.5 1.0 %copy-done.1 = bf16[128,2048]{1,0:T(8,128)(2,1)S(1)} copy-done((bf16[128,2048]{1,0:T(8,128)(2,1)S(1)}, bf16[128,2048]{1,0:T(8,128)(2,1)}, u32[]{:S(2)}) %copy-start.1) | copy-done | bytes 524312
  4.5 0.0 copy-start.2
  4.5 0.8 %copy-done.2 = bf16[128,256]{1,0:T(8,128)(2,1)S(1)} copy-done((bf16[128,256]{1,0:T(8,128)(2,1)S(1)}, bf16[128,256]{1,0:T(8,128)(2,1)}, u32[]{:S(2)}) %copy-start.2) | copy-done | bytes 65560
  5.3 0.0 copy-start.3
  5.4 0.8 %copy-done.3 = bf16[1,16,2048]{2,1,0:T(8,128)(2,1)S(1)} copy-done((bf16[1,16,2048]{2,1,0:T(8,128)(2,1)S(1)}, bf16[1,16,2048]{2,1,0:T(8,128)(2,1)}, u32[]{:S(2)}) %copy-start.3) | copy-done | bytes 65560
  6.2 0.0 copy-start.4
  6.2 0.7 %copy-done.4 = bf16[1,16,256]{2,1,0:T(8,128)(2,1)S(1)} copy-done((bf16[1,16,256]{2,1,0:T(8,128)(2,1)S(1)}, bf16[1,16,256]{2,1,0:T(8,128)(2,1)}, u32[]{:S(2)}) %copy-start.4) | copy-done | bytes 8216
  6.9 59.8 %shard_map.85 = (bf16[128,2048]{1,0:T(8,128)(2,1)S(1)}, f32[1,16,2048]{2,1,0:T(8,128)S(1)}, f32[1,16,256]{2,1,0:T(8,128)S(1)}) custom-call(bf16[128,2048]{1,0:T(8,128)(2,1)S(1)} %copy-done.1, bf16[128,256]{1,0:T(8,128)(2,1)S(1)} %copy-done.2, bf16[8192,256]{1,0:T(8,128)(2,1)S(1)} %copy-done, bf16[1,16,2048]{2,1,0:T(8,128)(2,1)S(1)} %copy-done.3, ...), custom_call_target="tpu_custom_call" | custom-call | tf_op jit(solution)/shard_map/pallas_call | solution.py:258
  66.7 0.8 %copy.13 = bf16[128,2048]{1,0:T(8,128)(2,1)} copy(bf16[128,2048]{1,0:T(8,128)(2,1)S(1)} %get-tuple-element.6) | data formatting | bytes 1048576
  67.5 0.7 copy.14
  68.2 0.6 copy.15
Async XLA Ops:
  1.3 2.2 %copy-start = (bf16[8192,256]{1,0:T(8,128)(2,1)S(1)}, bf16[8192,256]{1,0:T(8,128)(2,1)}, u32[]{:S(2)}) copy-start(bf16[8192,256]{1,0:T(8,128)(2,1)} %weight_hbm.1) | copy-start | bytes 12582916
  3.5 1.0 %copy-start.1 = (bf16[128,2048]{1,0:T(8,128)(2,1)S(1)}, bf16[128,2048]{1,0:T(8,128)(2,1)}, u32[]{:S(2)}) copy-start(bf16[128,2048]{1,0:T(8,128)(2,1)} %inputs_hbm.1) | copy-start | bytes 1572868
  4.5 0.8 %copy-start.2 = (bf16[128,256]{1,0:T(8,128)(2,1)S(1)}, bf16[128,256]{1,0:T(8,128)(2,1)}, u32[]{:S(2)}) copy-start(bf16[128,256]{1,0:T(8,128)(2,1)} %cot_ref.1) | copy-start | bytes 196612
  5.3 0.8 %copy-start.3 = (bf16[1,16,2048]{2,1,0:T(8,128)(2,1)S(1)}, bf16[1,16,2048]{2,1,0:T(8,128)(2,1)}, u32[]{:S(2)}) copy-start(bf16[1,16,2048]{2,1,0:T(8,128)(2,1)} %down_ref.1) | copy-start | bytes 196612
  6.2 0.7 %copy-start.4 = (bf16[1,16,256]{2,1,0:T(8,128)(2,1)S(1)}, bf16[1,16,256]{2,1,0:T(8,128)(2,1)}, u32[]{:S(2)}) copy-start(bf16[1,16,256]{2,1,0:T(8,128)(2,1)} %up_ref.1) | copy-start | bytes 24580

commit v2 on v1

--- a/solution.py
+++ b/solution.py
@@ -21,9 +21,9 @@
 
 
 def kernel(
-    inputs_hbm, cot_ref, weight_hbm, down_ref, up_ref, tenant_ref,
-    out_hbm, grad_down_ref, grad_up_ref,
-    xs, weight, partial, own, arrived, out_vm, cot_spread, pick,
+    inputs_hbm, cot_hbm, weight_hbm, down_hbm, up_hbm, tenant_ref,
+    out_hbm, grad_down_hbm, grad_up_hbm,
+    xs, cot_vm, weight, down_vm, up_vm, partial, own, arrived, out_vm, grad_down, grad_up, cot_spread, pick,
     s1, r1, r2, s3, r3, r4, s5, r5, s6, r6, s7, r7,
     load_sem, store_sem, send_sem, recv_sem, xsend_sem, xrecv_sem,
 ):
@@ -39,8 +39,14 @@
         h = lax.rem(y + k, Y)
         return h, (z * Y + h) * CORES + c
 
-    load_weight = pltpu.make_async_copy(weight_hbm, weight, load_sem.at[0])
-    load_inputs = pltpu.make_async_copy(inputs_hbm, xs, load_sem.at[1])
+    loads = [
+        pltpu.make_async_copy(src, dst, load_sem.at[i])
+        for i, (src, dst) in enumerate(
+            ((down_hbm, down_vm), (up_hbm, up_vm), (cot_hbm, cot_vm), (weight_hbm, weight), (inputs_hbm, xs))
+        )
+    ]
+    for load in loads:
+        load.start()
 
     barrier = pltpu.get_barrier_semaphore()
 
@@ -53,28 +59,16 @@
         pl.semaphore_signal(barrier, inc=1, device_id={"dp": y_member(k)[1]}, device_id_type=MESH)
         pl.semaphore_signal(barrier, inc=1, device_id={"tensor": lax.rem(mx + k, X)}, device_id_type=MESH)
 
-    load_weight.start()
-    load_inputs.start()
-
     lane0 = RANK * lax.rem(g, 8)
-    key = lax.broadcasted_iota(jnp.int32, (KEYS, KEYS), 0)
-    column = lax.broadcasted_iota(jnp.int32, (KEYS, KEYS), 1)
-    target = lax.div(key, RANK) * LANES + lax.rem(key, RANK) + lane0
-    lane = lax.broadcasted_iota(jnp.int32, (RANK, LANES), 1)
-    block_of_lane = lax.div(lane, RANK)
+    block_of_lane = lax.div(lax.broadcasted_iota(jnp.int32, (RANK, LANES), 1), RANK)
     tenant = jnp.full((RANK, LANES), tenant_ref[0], jnp.int32).astype(F32)
-    tenant = jnp.where(block_of_lane == lax.rem(g + 1, 8), tenant, 0.0)
-    cot = cot_ref[...]
-    up = up_ref[0]
-    for i in range(WIDTH // KEYS):
-        spread = (column + i * KEYS == target).astype(F32).astype(BF16)
-        cot_spread[:, i * KEYS : (i + 1) * KEYS] = dot(cot, spread).astype(BF16)
-        up_spread = dot(up, spread)
-        for q in range(2):
-            tile = up_spread[:, q * LANES : (q + 1) * LANES] + tenant
-            s1[2 * i + q, RANK:, :] = tile.astype(BF16)
+    loads[0].wait()
+    loads[1].wait()
+    up = up_vm[0].astype(F32)
     for q in range(G):
-        s1[q, :RANK, :] = down_ref[0, :, q * LANES : (q + 1) * LANES]
+        s1[q, :RANK, :] = down_vm[0, :, q * LANES : (q + 1) * LANES]
+        tile = up[:, q // 8 * LANES : (q // 8 + 1) * LANES]
+        s1[q, RANK:, :] = jnp.where(block_of_lane == q % 8, tile, tenant).astype(BF16)
 
     def group_exchange(step, src, dst):
         @pl.loop(0, G - 1)
@@ -90,8 +84,15 @@
     def received(step, dst):
         pltpu.make_async_copy(dst, dst, recv_sem.at[step]).wait()
 
-    load_weight.wait()
-    for k in range(X):
+    pl.semaphore_wait(barrier, G - 1 + Y - 1 + X - 1)
+
+    group_exchange(0, s1, r1)
+
+    loads[2].wait()
+    cot = cot_vm[...]
+    loads[3].wait()
+    shares = []
+    for k in (2, 1, 3, 0):
         q = lax.rem(mx + k, X)
 
         @pl.loop(0, WIDTH // KEYS)
@@ -104,26 +105,32 @@
             else:
                 partial[k - 1, :, columns] = product.astype(BF16)
 
-    load_inputs.wait()
-    pl.semaphore_wait(barrier, G - 1 + Y - 1 + X - 1)
-
-    group_exchange(0, s1, r1)
-    shares = []
-    for k in (2, 1, 3):
-        share = pltpu.make_async_remote_copy(
-            partial.at[k - 1], arrived.at[k - 1], xsend_sem.at[k - 1], xrecv_sem.at[k - 1],
-            device_id={"tensor": lax.rem(mx + k, X)}, device_id_type=MESH,
-        )
-        share.start()
-        shares.append(share)
+        if k > 0:
+            share = pltpu.make_async_remote_copy(
+                partial.at[k - 1], arrived.at[k - 1], xsend_sem.at[k - 1], xrecv_sem.at[k - 1],
+                device_id={"tensor": q}, device_id_type=MESH,
+            )
+            share.start()
+            shares.append(share)
+
+    key = lax.broadcasted_iota(jnp.int32, (KEYS, KEYS), 0)
+    column = lax.broadcasted_iota(jnp.int32, (KEYS, KEYS), 1)
+    target = lax.div(key, RANK) * LANES + lax.rem(key, RANK) + lane0
+    for i in range(WIDTH // KEYS):
+        spread = (column + i * KEYS == target).astype(F32).astype(BF16)
+        cot_spread[:, i * KEYS : (i + 1) * KEYS] = dot(cot, spread).astype(BF16)
+    loads[4].wait()
     received(0, r1)
 
     mine = r2.at[y]
     packed = [jnp.zeros((RANK, LANES), F32), jnp.zeros((RANK, LANES), F32)]
+    tenants = []
     for h in range(G):
         mine[h * RANK : (h + 1) * RANK, :] = r1[h, :RANK, :]
-        tile = r1[h, RANK:, :].astype(F32)
+        shift = lax.rem(RANK * (h % 8) + LANES - lane0, LANES)
+        tile = pltpu.roll(r1[h, RANK:, :].astype(F32), shift, 1)
         packed[h // 8] = jnp.where(block_of_lane == h % 8, tile, packed[h // 8])
+        tenants.append(tile)
     for q in range(2):
         mine[(G + q) * RANK : (G + q + 1) * RANK, :] = packed[q].astype(BF16)
     for k in (2, 1, 3):
@@ -136,7 +143,7 @@
     slot = lax.broadcasted_iota(jnp.int32, (RANK, Y * G * RANK), 1)
     for h in range(G):
         at = RANK * ((h + 1) % 8)
-        t = r1[h, RANK:, at : at + 1].astype(F32).astype(jnp.int32)
+        t = tenants[h][:, at : at + 1].astype(jnp.int32)
         t_y, t_g = (t >> 1) & 3, (t >> 3) * 2 + (t & 1)
         wanted = (t_y * G + t_g) * RANK + rank_row
         pick[h * RANK : (h + 1) * RANK, :] = (slot == wanted).astype(F32).astype(BF16)
@@ -228,20 +235,27 @@
         for k in range(X - 1):
             total += arrived[k, :, columns].astype(F32)
         out_vm[:, columns] = total.astype(BF16)
-    store_out = pltpu.make_async_copy(out_vm, out_hbm, store_sem)
-    store_out.start()
+    stores = [
+        pltpu.make_async_copy(src, dst, store_sem.at[i])
+        for i, (src, dst) in enumerate(((out_vm, out_hbm), (grad_down, grad_down_hbm), (grad_up, grad_up_hbm)))
+    ]
+    stores[0].start()
     received(6, r7)
 
     for h in range(G):
-        grad_down_ref[0, :, h * LANES : (h + 1) * LANES] = r7[h, :RANK, :]
+        grad_down[0, :, h * LANES : (h + 1) * LANES] = r7[h, :RANK, :]
+    stores[1].start()
     for q in range(2):
         total = jnp.zeros((RANK, LANES), F32)
         for h in range(8 * q, 8 * q + 8):
             moved = pltpu.roll(r7[h, RANK:, :], lax.rem(RANK * (h % 8) + LANES - lane0, LANES), 1)
             total = jnp.where(block_of_lane == h % 8, moved, total)
-        grad_up_ref[0, :, q * LANES : (q + 1) * LANES] = total
-
-    store_out.wait()
+        grad_up[0, :, q * LANES : (q + 1) * LANES] = total
+
+    stores[2].start()
+
+    for store in stores:
+        store.wait()
     for step, sent in ((0, s1), (2, s3), (4, s5), (6, s7)):
         peers = sent.at[pl.ds(0, G - 1)]
         pltpu.make_async_copy(peers, peers, send_sem.at[step]).wait()
@@ -252,7 +266,6 @@
 
 def on_device(inputs, cotangent, frozen_key_weight, adapter_down_weight, adapter_up_weight, tenant_per_block):
     hbm = pl.BlockSpec(memory_space=pl.ANY)
-    vmem = pl.BlockSpec(memory_space=pltpu.VMEM)
     smem = pl.BlockSpec(memory_space=pltpu.SMEM)
     dma = pltpu.SemaphoreType.DMA
     return pl.pallas_call(
@@ -262,15 +275,20 @@
             jax.ShapeDtypeStruct((1, RANK, WIDTH), F32),
             jax.ShapeDtypeStruct((1, RANK, KEYS), F32),
         ),
-        in_specs=[hbm, vmem, hbm, vmem, vmem, smem],
-        out_specs=(hbm, vmem, vmem),
+        in_specs=[hbm] * 5 + [smem],
+        out_specs=(hbm, hbm, hbm),
         scratch_shapes=[
             pltpu.VMEM((ROWS, WIDTH), BF16),
+            pltpu.VMEM((ROWS, KEYS), BF16),
             pltpu.VMEM((X * WIDTH, KEYS), BF16),
+            pltpu.VMEM((1, RANK, WIDTH), BF16),
+            pltpu.VMEM((1, RANK, KEYS), BF16),
             pltpu.VMEM((X - 1, ROWS, WIDTH), BF16),
             pltpu.VMEM((ROWS, WIDTH), F32),
             pltpu.VMEM((X - 1, ROWS, WIDTH), BF16),
             pltpu.VMEM((ROWS, WIDTH), BF16),
+            pltpu.VMEM((1, RANK, WIDTH), F32),
+            pltpu.VMEM((1, RANK, KEYS), F32),
             pltpu.VMEM((ROWS, WIDTH), BF16),
             pltpu.VMEM((G * RANK, Y * G * RANK), BF16),
             pltpu.VMEM((G, 2 * RANK, LANES), BF16),
@@ -285,10 +303,10 @@
             pltpu.VMEM((Y, TABLE, LANES), BF16),
             pltpu.VMEM((G, 2 * RANK, LANES), F32),
             pltpu.VMEM((G, 2 * RANK, LANES), F32),
-            dma((2,)), dma, dma((7,)), dma((7,)), dma((X - 1,)), dma((X - 1,)),
+            dma((5,)), dma((3,)), dma((7,)), dma((7,)), dma((X - 1,)), dma((X - 1,)),
         ],
         compiler_params=pltpu.CompilerParams(
-            collective_id=0, has_side_effects=True, vmem_limit_bytes=40 << 20
+            collective_id=0, has_side_effects=True, vmem_limit_bytes=60 << 20
         ),
     )(inputs, cotangent, frozen_key_weight, adapter_down_weight, adapter_up_weight, tenant_per_block)
 

time: 69.1 us -> 64.9 us (0.939)
  local copies, waits for them, and re-layouts: 7.65 us -> 4.77 us
  Pallas kernels: 59.8 us -> 58.7 us
    unnamed x13 -> x3, local copies, waits for them, and re-layouts: 7.65 us -> 4.77 us
    pallas_call x1, Pallas kernels: 59.8 us -> 58.7 us  [on_device(): pl.pallas_call(kernel, out_shape=(jax.ShapeDtypeStruct((ROWS, WIDTH), BF1...]
where the time goes in v2:
time: 64.9 us; the launch traced here: 64.7 us
  Pallas kernels  58.7 us (90%)
  local copies, waits for them, and re-layouts  4.77 us (7%)
  between operations  1.29 us (2%)
    pallas_call x1, Pallas kernels, on_device(): pl.pallas_call(kernel, out_shape=(jax.ShapeDtypeStruct((ROWS, WIDTH), BF1...  58.7 us
    unnamed x3, local copies, waits for them, and re-layouts  4.77 us

profile of v2, /device:TPU:1, one launch (start us, length us, event | category | flops | bytes accessed | tf_op | source)
XLA Modules:
  0.0 64.7 jit_solution(5095031879437686767)
XLA Ops:
  1.3 58.7 %shard_map.85 = (bf16[128,2048]{1,0:T(8,128)(2,1)}, f32[1,16,2048]{2,1,0:T(8,128)}, f32[1,16,256]{2,1,0:T(8,128)}) custom-call(bf16[128,2048]{1,0:T(8,128)(2,1)} %inputs_hbm.1, bf16[128,256]{1,0:T(8,128)(2,1)} %cot_hbm.1, bf16[8192,256]{1,0:T(8,128)(2,1)} %weight_hbm.1, bf16[1,16,2048]{2,1,0:T(8,128)(2,1)} %down_hbm.1, bf16[1,16,256]{2,1,0:T(8,128)(2,1)} %up_hbm.1, ...), custom_call_target="tpu_custom_call" | custom-call | tf_op jit(solution)/shard_map/pallas_call | solution.py:271
  60.0 1.9 %copy.13 = bf16[128,2048]{1,0:T(8,128)(2,1)} copy(bf16[128,2048]{1,0:T(8,128)(2,1)} %get-tuple-element.6) | data formatting | bytes 1048576
  61.8 1.6 %copy.14 = f32[1,16,2048]{2,1,0:T(8,128)} copy(f32[1,16,2048]{2,1,0:T(8,128)} %get-tuple-element.7) | data formatting | bytes 262144
  63.4 1.3 %copy.15 = f32[1,16,256]{2,1,0:T(8,128)} copy(f32[1,16,256]{2,1,0:T(8,128)} %get-tuple-element.8) | data formatting | bytes 32768

commit v3 on v2

--- a/solution.py
+++ b/solution.py
@@ -24,7 +24,7 @@
     inputs_hbm, cot_hbm, weight_hbm, down_hbm, up_hbm, tenant_ref,
     out_hbm, grad_down_hbm, grad_up_hbm,
     xs, cot_vm, weight, down_vm, up_vm, partial, own, arrived, out_vm, grad_down, grad_up, cot_spread, pick,
-    s1, r1, r2, s3, r3, r4, s5, r5, s6, r6, s7, r7,
+    s1, r1, r2, s3, r3, r4, s5, r5, s6, r6, s7, r7, s7u, r7u,
     load_sem, store_sem, send_sem, recv_sem, xsend_sem, xrecv_sem,
 ):
     me, mx = lax.axis_index("dp"), lax.axis_index("tensor")
@@ -92,26 +92,21 @@
     cot = cot_vm[...]
     loads[3].wait()
     shares = []
-    for k in (2, 1, 3, 0):
+    for k in (1, 3, 2, 0):
         q = lax.rem(mx + k, X)
-
-        @pl.loop(0, WIDTH // KEYS)
-        def _(i):
-            at = pl.multiple_of(q * WIDTH + i * KEYS, KEYS)
-            product = dot(cot, weight[pl.ds(at, KEYS), :], ((1,), (1,)))
-            columns = pl.ds(pl.multiple_of(i * KEYS, KEYS), KEYS)
-            if k == 0:
-                own[:, columns] = product
-            else:
-                partial[k - 1, :, columns] = product.astype(BF16)
-
-        if k > 0:
-            share = pltpu.make_async_remote_copy(
-                partial.at[k - 1], arrived.at[k - 1], xsend_sem.at[k - 1], xrecv_sem.at[k - 1],
-                device_id={"tensor": q}, device_id_type=MESH,
+        product = dot(cot, weight[pl.ds(pl.multiple_of(q * WIDTH, WIDTH), WIDTH), :], ((1,), (1,)))
+        if k == 0:
+            own[...] = product
+        else:
+            partial[k - 1] = product.astype(BF16)
+            shares.append(
+                pltpu.make_async_remote_copy(
+                    partial.at[k - 1], arrived.at[k - 1], xsend_sem.at[k - 1], xrecv_sem.at[k - 1],
+                    device_id={"tensor": q}, device_id_type=MESH,
+                )
             )
-            share.start()
-            shares.append(share)
+            if k != 2:
+                shares[-1].start()
 
     key = lax.broadcasted_iota(jnp.int32, (KEYS, KEYS), 0)
     column = lax.broadcasted_iota(jnp.int32, (KEYS, KEYS), 1)
@@ -175,6 +170,7 @@
             r4.at[mx], r4.at[mx], send_sem.at[3], recv_sem.at[3],
             device_id={"tensor": lax.rem(mx + k, X)}, device_id_type=MESH,
         ).start()
+    shares[2].start()
     others = r4.at[pl.ds(0, X - 1)]
     pltpu.make_async_copy(others, others, recv_sem.at[3]).wait()
     low = ((r4[0] + r4[1]) + (r4[2] + r4[3])).astype(BF16)
@@ -215,17 +211,27 @@
     pltpu.make_async_copy(s6.at[y], r6.at[y], recv_sem.at[5]).start()
     received(5, r6)
 
+    half = RANK // 2
+    row = lax.broadcasted_iota(jnp.int32, (half, LANES), 0)
+    block = lax.div(lax.broadcasted_iota(jnp.int32, (half, LANES), 1), RANK)
     for h in range(G + 2):
         rows = slice(h * RANK, (h + 1) * RANK)
         total = (r6[0, rows, :].astype(F32) + r6[1, rows, :].astype(F32)) + (
             r6[2, rows, :].astype(F32) + r6[3, rows, :].astype(F32)
         )
         if h < G:
-            s7[h, :RANK, :] = total
-        else:
-            for owner in range(8 * (h - G), 8 * (h - G) + 8):
-                s7[owner, RANK:, :] = total
+            s7[h] = total
+            continue
+        for i in range(2):
+            ranks = total[half * i : half * (i + 1)]
+            turned = ranks
+            for j in range(1, half):
+                turned = jnp.where(row == j, pltpu.roll(ranks, j * RANK, 1), turned)
+            for j in range(half):
+                chosen = jnp.where(block == lax.rem(row + j, half), turned, 0.0)
+                s7u[half * (h - G) + j, i : i + 1, :] = jnp.sum(chosen, axis=0, keepdims=True)
     group_exchange(6, s7, r7)
+    group_exchange(7, s7u, r7u)
 
     for share in shares:
         share.wait()
@@ -245,18 +251,24 @@
     for h in range(G):
         grad_down[0, :, h * LANES : (h + 1) * LANES] = r7[h, :RANK, :]
     stores[1].start()
+    received(7, r7u)
+    mine = block == lax.rem(row + lax.rem(g, half), half)
     for q in range(2):
-        total = jnp.zeros((RANK, LANES), F32)
-        for h in range(8 * q, 8 * q + 8):
-            moved = pltpu.roll(r7[h, RANK:, :], lax.rem(RANK * (h % 8) + LANES - lane0, LANES), 1)
-            total = jnp.where(block_of_lane == h % 8, moved, total)
-        grad_up[0, :, q * LANES : (q + 1) * LANES] = total
-
+        for i in range(2):
+            turned = jnp.zeros((half, LANES), F32)
+            for h in range(half):
+                value = jnp.broadcast_to(r7u[half * q + h, i : i + 1, :], (half, LANES))
+                turned += pltpu.roll(jnp.where(mine, value, 0.0), h * RANK, 1)
+            turned = pltpu.roll(turned, lax.rem(LANES - lane0, LANES), 1)
+            total = turned
+            for j in range(1, half):
+                total = jnp.where(row == j, pltpu.roll(turned, LANES - j * RANK, 1), total)
+            grad_up[0, half * i : half * (i + 1), q * LANES : (q + 1) * LANES] = total
     stores[2].start()
 
     for store in stores:
         store.wait()
-    for step, sent in ((0, s1), (2, s3), (4, s5), (6, s7)):
+    for step, sent in ((0, s1), (2, s3), (4, s5), (6, s7), (7, s7u)):
         peers = sent.at[pl.ds(0, G - 1)]
         pltpu.make_async_copy(peers, peers, send_sem.at[step]).wait()
     for step, sent in ((1, r2), (3, r4), (5, s6)):
@@ -301,9 +313,11 @@
             pltpu.VMEM((G, 2 * RANK, LANES), BF16),
             pltpu.VMEM((Y, TABLE, LANES), BF16),
             pltpu.VMEM((Y, TABLE, LANES), BF16),
-            pltpu.VMEM((G, 2 * RANK, LANES), F32),
-            pltpu.VMEM((G, 2 * RANK, LANES), F32),
-            dma((5,)), dma((3,)), dma((7,)), dma((7,)), dma((X - 1,)), dma((X - 1,)),
+            pltpu.VMEM((G, RANK, LANES), F32),
+            pltpu.VMEM((G, RANK, LANES), F32),
+            pltpu.VMEM((G, 2, LANES), F32),
+            pltpu.VMEM((G, 2, LANES), F32),
+            dma((5,)), dma((3,)), dma((8,)), dma((8,)), dma((X - 1,)), dma((X - 1,)),
         ],
         compiler_params=pltpu.CompilerParams(
             collective_id=0, has_side_effects=True, vmem_limit_bytes=60 << 20

time: 64.9 us -> 64.8 us (level)
  no operation moved by 1% of the time
where the time goes in v3:
time: 64.8 us; the launch traced here: 64.6 us
  Pallas kernels  58.5 us (90%)
  local copies, waits for them, and re-layouts  4.77 us (7%)
  between operations  1.29 us (2%)
    pallas_call x1, Pallas kernels, on_device(): pl.pallas_call(kernel, out_shape=(jax.ShapeDtypeStruct((ROWS, WIDTH), BF1...  58.5 us
    unnamed x3, local copies, waits for them, and re-layouts  4.77 us

profile of v3, /device:TPU:1, one launch (start us, length us, event | category | flops | bytes accessed | tf_op | source)
XLA Modules:
  0.0 64.6 jit_solution(16724699096157105966)
XLA Ops:
  1.3 58.5 %shard_map.85 = (bf16[128,2048]{1,0:T(8,128)(2,1)}, f32[1,16,2048]{2,1,0:T(8,128)}, f32[1,16,256]{2,1,0:T(8,128)}) custom-call(bf16[128,2048]{1,0:T(8,128)(2,1)} %inputs_hbm.1, bf16[128,256]{1,0:T(8,128)(2,1)} %cot_hbm.1, bf16[8192,256]{1,0:T(8,128)(2,1)} %weight_hbm.1, bf16[1,16,2048]{2,1,0:T(8,128)(2,1)} %down_hbm.1, bf16[1,16,256]{2,1,0:T(8,128)(2,1)} %up_hbm.1, ...), custom_call_target="tpu_custom_call" | custom-call | tf_op jit(solution)/shard_map/pallas_call | solution.py:283
  59.8 1.9 %copy.13 = bf16[128,2048]{1,0:T(8,128)(2,1)} copy(bf16[128,2048]{1,0:T(8,128)(2,1)} %get-tuple-element.6) | data formatting | bytes 1048576
  61.7 1.6 %copy.14 = f32[1,16,2048]{2,1,0:T(8,128)} copy(f32[1,16,2048]{2,1,0:T(8,128)} %get-tuple-element.7) | data formatting | bytes 262144
  63.3 1.3 %copy.15 = f32[1,16,256]{2,1,0:T(8,128)} copy(f32[1,16,256]{2,1,0:T(8,128)} %get-tuple-element.8) | data formatting | bytes 32768

commit v4 on v0

v4 whole, which is shorter than its diff:
```python
import jax
import jax.numpy as jnp
from jax import lax
from jax.experimental import pallas as pl
from jax.experimental.pallas import tpu as pltpu
from jax.sharding import PartitionSpec as P

MESH = pl.DeviceIdType.MESH
F32 = jnp.float32
BF16 = jnp.bfloat16
ADAPTER_SCALE = 2.0

Z, Y, CORES, X = 8, 4, 2, 4
G = Z * CORES
ROWS, WIDTH, KEYS, RANK, LANES = 128, 2048, 256, 16, 128
HALF, SPLIT = 64, 80

STEPS = 14
UP_ALL, ID_Y, DOWN_IN, ID_G, UP_PICK, DOWN_ALL, OUT_SUM, DOWN_PICK, TERM, IN_SUM, TERM_Y, UP_TERM, TERM_OWNER, UP_TERM_Y = range(STEPS)


def dot(a, b, dims=((1,), (0,))):
    return lax.dot_general(a, b, (dims, ((), ())), preferred_element_type=F32)


def kernel(
    inputs_hbm, cot_hbm, weight_hbm, down_hbm, up_hbm, tenant_ref,
    out_ref, grad_down_ref, grad_up_ref,
    xs, cot_vm, weight, down_vm, up_vm, partial, own, arrived, hop, ids, pick,
    up_all, id_y, down_in, down_all, id_g, up_send, up_recv, out_sum, down_send, down_recv, in_sum,
    term_send, term_recv, term_y_send, term_y_recv, term_owner_send, term_owner_recv,
    up_term, up_term_all, up_term_y_send, up_term_y_recv,
    load_sem, send_sem, recv_sem, xsend_sem, xrecv_sem,
):
    me, mx = lax.axis_index("dp"), lax.axis_index("tensor")
    z, y, c = lax.div(me, Y * CORES), lax.rem(lax.div(me, CORES), Y), lax.rem(me, CORES)
    g = z * CORES + c
    x_next, x_last = lax.rem(mx + 1, X), lax.rem(mx + X - 1, X)

    def group_member(i):
        h = lax.rem(g + G // 2 + (1 - 2 * lax.rem(i, 2)) * lax.div(i + 1, 2), G)
        return h, (lax.div(h, CORES) * Y + y) * CORES + lax.rem(h, CORES)

    def y_member(k):
        h = lax.rem(y + k, Y)
        return h, (z * Y + h) * CORES + c

    def send(step, src, dst, axis, device):
        pltpu.make_async_remote_copy(
            src, dst, send_sem.at[step], recv_sem.at[step], device_id={axis: device}, device_id_type=MESH
        ).start()

    def keep(step, src, dst):
        pltpu.make_async_copy(src, dst, recv_sem.at[step]).start()

    def received(step, dst):
        pltpu.make_async_copy(dst, dst, recv_sem.at[step]).wait()

    loads = [
        pltpu.make_async_copy(src, dst, load_sem.at[i])
        for i, (src, dst) in enumerate(
            ((up_hbm, up_vm), (down_hbm, down_vm), (cot_hbm, cot_vm), (weight_hbm, weight), (inputs_hbm, xs))
        )
    ]
    for load in loads:
        load.start()

    barrier = pltpu.get_barrier_semaphore()

    @pl.loop(0, G - 1)
    def _(i):
        _, device = group_member(i)
        pl.semaphore_signal(barrier, inc=1, device_id={"dp": device}, device_id_type=MESH)

    for k in (2, 1, 3):
        pl.semaphore_signal(barrier, inc=1, device_id={"dp": y_member(k)[1]}, device_id_type=MESH)
        pl.semaphore_signal(barrier, inc=1, device_id={"tensor": lax.rem(mx + k, X)}, device_id_type=MESH)

    ids[0] = jnp.full((1, LANES), tenant_ref[0], jnp.int32).astype(F32)
    loads[0].wait()
    loads[1].wait()
    for q in range(G):
        down_in[q] = down_vm[0, :, q * LANES : (q + 1) * LANES]
    pl.semaphore_wait(barrier, G - 1 + Y - 1 + X - 1)

    @pl.loop(0, G - 1)
    def _(i):
        send(UP_ALL, up_vm.at[0], up_all.at[g], "dp", group_member(i)[1])

    keep(UP_ALL, up_vm.at[0], up_all.at[g])
    for k in (2, 1, 3):
        send(ID_Y, ids.at[0], id_y.at[y], "dp", y_member(k)[1])
    keep(ID_Y, ids.at[0], id_y.at[y])
    my_rows = pl.ds(pl.multiple_of(g * RANK, RANK), RANK)

    @pl.loop(0, G - 1)
    def _(i):
        h, device = group_member(i)
        send(DOWN_IN, down_in.at[h], down_all.at[y, my_rows], "dp", device)

    keep(DOWN_IN, down_in.at[g], down_all.at[y, my_rows])

    @pl.loop(0, G - 1)
    def _(i):
        send(ID_G, ids.at[0], id_g.at[g], "dp", group_member(i)[1])

    keep(ID_G, ids.at[0], id_g.at[g])

    def share(i, src, dst, device):
        return pltpu.make_async_remote_copy(
            src, dst, xsend_sem.at[i], xrecv_sem.at[i], device_id={"tensor": device}, device_id_type=MESH
        )

    low_half, high_half = pl.ds(0, HALF), pl.ds(HALF, ROWS - HALF)
    first, rest = pl.ds(0, SPLIT), pl.ds(SPLIT, ROWS - SPLIT)
    hops = (
        share(0, partial.at[1, low_half], hop.at[0], x_next),
        share(1, partial.at[1, high_half], hop.at[1], x_last),
    )
    nearby = (
        share(2, partial.at[0, first], arrived.at[0, first], x_next),
        share(3, partial.at[2, first], arrived.at[2, first], x_last),
    )
    last = (
        share(4, partial.at[0, rest], arrived.at[0, rest], x_next),
        share(5, partial.at[2, rest], arrived.at[2, rest], x_last),
        share(6, hop.at[0], arrived.at[1, low_half], x_next),
        share(7, hop.at[1], arrived.at[1, high_half], x_last),
    )
    loads[2].wait()
    cot = cot_vm[...]
    loads[3].wait()
    for k in (2, 1, 3, 0):
        at = pl.multiple_of(lax.rem(mx + k, X) * WIDTH, WIDTH)
        product = dot(cot, weight[pl.ds(at, WIDTH), :], ((1,), (1,)))
        if k == 0:
            own[...] = product
        else:
            partial[k - 1] = product.astype(BF16)
        if k == 2:
            for copy in hops:
                copy.start()

    def place(t):
        t = t.astype(jnp.int32)
        return (t >> 1) & 3, (t >> 3) * CORES + (t & 1)

    rank = lax.broadcasted_iota(jnp.int32, (RANK, 1), 0)
    slot = lax.broadcasted_iota(jnp.int32, (RANK, G * RANK), 1)
    received(ID_Y, id_y)
    wanted = []
    for h in range(Y):
        t_y, t_g = place(jnp.broadcast_to(id_y[h, :, :1], (RANK, 1)))
        wanted.append((slot == jnp.where(t_y == y, t_g * RANK + rank, -1)).astype(F32).astype(BF16))
    wanted = jnp.concatenate(wanted, axis=0)
    received(UP_ALL, up_all)
    chosen = dot(wanted, up_all[...].reshape(G * RANK, KEYS)).astype(BF16)
    for h in range(Y):
        up_send[h] = chosen[h * RANK : (h + 1) * RANK]
    for k in (2, 1, 3):
        h, device = y_member(k)
        send(UP_PICK, up_send.at[h], up_recv.at[y], "dp", device)
    keep(UP_PICK, up_send.at[y], up_recv.at[y])

    received(DOWN_IN, down_all.at[y])
    for k in (2, 1, 3):
        send(DOWN_ALL, down_all.at[y], down_all.at[y], "dp", y_member(k)[1])

    received(ID_G, id_g)
    slot = lax.broadcasted_iota(jnp.int32, (RANK, Y * G * RANK), 1)
    column = lax.broadcasted_iota(jnp.int32, (RANK, Y * RANK), 1)
    mine = []
    for h in range(G):
        t_y, t_g = place(jnp.broadcast_to(id_g[h, :, :1], (RANK, 1)))
        pick[h * RANK : (h + 1) * RANK, :] = (slot == (t_y * G + t_g) * RANK + rank).astype(F32).astype(BF16)
        mine.append((column == jnp.where(t_g == g, t_y * RANK + rank, -1)).astype(F32).astype(BF16))
    mine = jnp.concatenate(mine, axis=0)

    def pick_of(q):
        return pick[:, q * G * RANK : (q + 1) * G * RANK]

    received(UP_PICK, up_recv)
    up_b = (up_recv[0].astype(F32) + up_recv[1].astype(F32)) + (up_recv[2].astype(F32) + up_recv[3].astype(F32))
    out_sum[mx] = ADAPTER_SCALE * dot(up_b.astype(BF16), cot, ((1,), (1,)))
    for k in (2, 1, 3):
        send(OUT_SUM, out_sum.at[mx], out_sum.at[mx], "tensor", lax.rem(mx + k, X))
    for copy in nearby:
        copy.start()

    received(DOWN_ALL, down_all.at[pl.ds(0, Y - 1)])
    tiles = jnp.zeros((G * RANK, LANES), F32)
    for q in range(Y):
        tiles += dot(pick_of(q), down_all[q])
    for h in range(G):
        down_send[h] = tiles[h * RANK : (h + 1) * RANK].astype(BF16)

    @pl.loop(0, G - 1)
    def _(i):
        h, device = group_member(i)
        send(DOWN_PICK, down_send.at[h], down_recv.at[g], "dp", device)

    keep(DOWN_PICK, down_send.at[g], down_recv.at[g])

    loads[4].wait()
    received(OUT_SUM, out_sum.at[pl.ds(0, X - 1)])
    low_out = ((out_sum[0] + out_sum[1]) + (out_sum[2] + out_sum[3])).astype(BF16)
    term = dot(low_out, xs[...]).astype(BF16)
    for h in range(G):
        term_send[h] = term[:, h * LANES : (h + 1) * LANES]

    @pl.loop(0, G - 1)
    def _(i):
        h, device = group_member(i)
        send(TERM, term_send.at[h], term_recv.at[g], "dp", device)

    keep(TERM, term_send.at[g], term_recv.at[g])

    received(DOWN_PICK, down_recv)
    down_b = jnp.concatenate([down_recv[h] for h in range(G)], axis=1)
    in_sum[mx] = dot(down_b, xs[...], ((1,), (1,)))
    for k in (2, 1, 3):
        send(IN_SUM, in_sum.at[mx], in_sum.at[mx], "tensor", lax.rem(mx + k, X))
    for copy in hops:
        copy.wait_recv()
    for copy in last:
        copy.start()
    own[...] += dot(low_out, down_b, ((0,), (0,)))

    received(TERM, term_recv)
    terms = term_recv[...].reshape(G * RANK, LANES)
    for q in range(Y):
        term_y_send[q] = dot(pick_of(q), terms, ((0,), (0,))).astype(BF16)
    for k in (2, 1, 3):
        h, device = y_member(k)
        send(TERM_Y, term_y_send.at[h], term_y_recv.at[y], "dp", device)
    keep(TERM_Y, term_y_send.at[y], term_y_recv.at[y])

    received(IN_SUM, in_sum.at[pl.ds(0, X - 1)])
    low_in = ((in_sum[0] + in_sum[1]) + (in_sum[2] + in_sum[3])).astype(BF16)
    up_term[...] = (ADAPTER_SCALE * dot(low_in, cot)).astype(BF16)

    @pl.loop(0, G - 1)
    def _(i):
        send(UP_TERM, up_term, up_term_all.at[g], "dp", group_member(i)[1])

    keep(UP_TERM, up_term, up_term_all.at[g])

    received(TERM_Y, term_y_recv)
    for h in range(G):
        rows = slice(h * RANK, (h + 1) * RANK)
        term_owner_send[h] = (term_y_recv[0, rows].astype(F32) + term_y_recv[1, rows].astype(F32)) + (
            term_y_recv[2, rows].astype(F32) + term_y_recv[3, rows].astype(F32)
        )

    @pl.loop(0, G - 1)
    def _(i):
        h, device = group_member(i)
        send(TERM_OWNER, term_owner_send.at[h], term_owner_recv.at[g], "dp", device)

    keep(TERM_OWNER, term_owner_send.at[g], term_owner_recv.at[g])

    received(UP_TERM, up_term_all)
    sums = dot(mine, up_term_all[...].reshape(G * RANK, KEYS), ((0,), (0,)))
    for h in range(Y):
        up_term_y_send[h] = sums[h * RANK : (h + 1) * RANK]
    for k in (2, 1, 3):
        h, device = y_member(k)
        send(UP_TERM_Y, up_term_y_send.at[h], up_term_y_recv.at[y], "dp", device)
    keep(UP_TERM_Y, up_term_y_send.at[y], up_term_y_recv.at[y])

    for copy in nearby + last:
        copy.wait_recv()
    for i in range(WIDTH // KEYS):
        columns = slice(i * KEYS, (i + 1) * KEYS)
        total = own[:, columns]
        for k in range(X - 1):
            total += arrived[k, :, columns].astype(F32)
        out_ref[:, columns] = total.astype(BF16)
    received(TERM_OWNER, term_owner_recv)
    for h in range(G):
        grad_down_ref[0, :, h * LANES : (h + 1) * LANES] = term_owner_recv[h]
    received(UP_TERM_Y, up_term_y_recv)
    grad_up_ref[0] = (up_term_y_recv[0] + up_term_y_recv[1]) + (up_term_y_recv[2] + up_term_y_recv[3])

    for copy in hops + nearby + last:
        copy.wait_send()
    for step, sent, peers in (
        (UP_ALL, up_all, G - 1), (ID_Y, id_y, Y - 1), (DOWN_IN, down_in, G - 1), (ID_G, id_g, G - 1),
        (UP_PICK, up_send, Y - 1), (DOWN_ALL, down_all, Y - 1), (OUT_SUM, out_sum, X - 1),
        (DOWN_PICK, down_send, G - 1), (TERM, term_send, G - 1), (IN_SUM, in_sum, X - 1),
        (TERM_Y, term_y_send, Y - 1), (UP_TERM, up_term_all, G - 1), (TERM_OWNER, term_owner_send, G - 1),
        (UP_TERM_Y, up_term_y_send, Y - 1),
    ):
        view = sent.at[pl.ds(0, peers)]
        pltpu.make_async_copy(view, view, send_sem.at[step]).wait()


def store_kernel(out_vm, grad_down_vm, grad_up_vm, out_hbm, grad_down_hbm, grad_up_hbm, sem):
    copies = [
        pltpu.make_async_copy(src, dst, sem.at[i])
        for i, (src, dst) in enumerate(
            ((out_vm, out_hbm), (grad_down_vm, grad_down_hbm), (grad_up_vm, grad_up_hbm))
        )
    ]
    for copy in copies:
        copy.start()
    for copy in copies:
        copy.wait()


def on_device(inputs, cotangent, frozen_key_weight, adapter_down_weight, adapter_up_weight, tenant_per_block):
    hbm = pl.BlockSpec(memory_space=pltpu.HBM)
    anywhere = pl.BlockSpec(memory_space=pl.ANY)
    vmem = pl.BlockSpec(memory_space=pltpu.VMEM)
    smem = pl.BlockSpec(memory_space=pltpu.SMEM)
    dma = pltpu.SemaphoreType.DMA
    results = (
        jax.ShapeDtypeStruct((ROWS, WIDTH), BF16),
        jax.ShapeDtypeStruct((1, RANK, WIDTH), F32),
        jax.ShapeDtypeStruct((1, RANK, KEYS), F32),
    )
    held = pl.pallas_call(
        kernel,
        out_shape=tuple(pltpu.VMEM(r.shape, r.dtype) for r in results),
        in_specs=[hbm] * 5 + [smem],
        out_specs=(vmem, vmem, vmem),
        scratch_shapes=[
            pltpu.VMEM((ROWS, WIDTH), BF16),
            pltpu.VMEM((ROWS, KEYS), BF16),
            pltpu.VMEM((X * WIDTH, KEYS), BF16),
            pltpu.VMEM((1, RANK, WIDTH), BF16),
            pltpu.VMEM((1, RANK, KEYS), BF16),
            pltpu.VMEM((X - 1, ROWS, WIDTH), BF16),
            pltpu.VMEM((ROWS, WIDTH), F32),
            pltpu.VMEM((X - 1, ROWS, WIDTH), BF16),
            pltpu.VMEM((2, HALF, WIDTH), BF16),
            pltpu.VMEM((1, 1, LANES), F32),
            pltpu.VMEM((G * RANK, Y * G * RANK), BF16),
            pltpu.VMEM((G, RANK, KEYS), BF16),
            pltpu.VMEM((Y, 1, LANES), F32),
            pltpu.VMEM((G, RANK, LANES), BF16),
            pltpu.VMEM((Y, G * RANK, LANES), BF16),
            pltpu.VMEM((G, 1, LANES), F32),
            pltpu.VMEM((Y, RANK, KEYS), BF16),
            pltpu.VMEM((Y, RANK, KEYS), BF16),
            pltpu.VMEM((X, RANK, ROWS), F32),
            pltpu.VMEM((G, RANK, LANES), BF16),
            pltpu.VMEM((G, RANK, LANES), BF16),
            pltpu.VMEM((X, RANK, ROWS), F32),
            pltpu.VMEM((G, RANK, LANES), BF16),
            pltpu.VMEM((G, RANK, LANES), BF16),
            pltpu.VMEM((Y, G * RANK, LANES), BF16),
            pltpu.VMEM((Y, G * RANK, LANES), BF16),
            pltpu.VMEM((G, RANK, LANES), F32),
            pltpu.VMEM((G, RANK, LANES), F32),
            pltpu.VMEM((RANK, KEYS), BF16),
            pltpu.VMEM((G, RANK, KEYS), BF16),
            pltpu.VMEM((Y, RANK, KEYS), F32),
            pltpu.VMEM((Y, RANK, KEYS), F32),
            dma((5,)), dma((STEPS,)), dma((STEPS,)), dma((8,)), dma((8,)),
        ],
        compiler_params=pltpu.CompilerParams(
            collective_id=0, has_side_effects=True, vmem_limit_bytes=60 << 20
        ),
    )(inputs, cotangent, frozen_key_weight, adapter_down_weight, adapter_up_weight, tenant_per_block)
    return pl.pallas_call(
        store_kernel,
        out_shape=results,
        in_specs=[anywhere] * 3,
        out_specs=(anywhere, anywhere, anywhere),
        scratch_shapes=[dma((3,))],
        compiler_params=pltpu.CompilerParams(vmem_limit_bytes=1 << 20),
    )(*held)


def solution(mesh):
    in_specs = (
        P("dp", "tensor"),
        P("dp", "tensor"),
        P(None, "tensor"),
        P("dp", None, "tensor"),
        P("dp", None, "tensor"),
        P("dp"),
    )
    out_specs = (P("dp", "tensor"), P("dp", None, "tensor"), P("dp", None, "tensor"))
    return jax.shard_map(
        on_device, mesh=mesh, in_specs=in_specs, out_specs=out_specs, check_vma=False
    )
```

time: 345 us -> 44.7 us (0.13)
  waiting for transfers between devices: 226 us -> 0 us
  blocking collectives: 68 us -> 0 us
  Pallas kernels: 0 us -> 43.3 us
  matrix products: 20.2 us -> 0 us
  between operations: 16.2 us -> 1.29 us
  other arithmetic: 8.11 us -> 0 us
  local copies, waits for them, and re-layouts: 5.65 us -> 0 us
    unnamed x4 -> x0, waiting for transfers between devices: 201 us -> none
    all_gather x1 -> x0, blocking collectives: 54.9 us -> none  [on_device(): lax.all_gather(adapter_up_weight, 'dp', axis=0, tiled=True)]
    pallas_call x0 -> x2, Pallas kernels: none -> 43.3 us  [the longest x1 42.4 us: on_device(): pl.pallas_call(kernel, out_shape=tuple((pltpu.VMEM(r.shape, r.dtype) for...]
    all_gather x1 -> x0, waiting for transfers between devices: 24.5 us -> none  [on_device(): lax.all_gather(adapter_down_weight, 'dp', axis=0, tiled=True)]
    dot_general x8 -> x0, matrix products: 20.2 us -> none  [the longest x1 6.7 us: on_device(): jnp.einsum('bk,krd->brd', member, pieces[0], preferred_element_type=jnp.f...]
    psum x1 -> x0, blocking collectives: 13.1 us -> none  [on_device(): low_in, reduced_output = lax.psum((low_in, reduced_output), 'tensor')]
    concatenate x1 -> x0, other arithmetic: 7.91 us -> none  [on_device(): combined = jnp.concatenate([down_contribution, up_contribution], axis=2)]
    slice x2 -> x0, local copies, waits for them, and re-layouts: 4.22 us -> none  [the longest x1 2.19 us: on_device(): grad_down = owned[:, :, :width_portion]]
  transfers between devices with their start and end apart: 3 -> 0, of which waited for: 2 -> 0; matrix products, arithmetic and copies ran while one was open for 8% -> 0% of each run, Pallas kernels for 0% -> 0%
where the time goes in v4:
time: 44.7 us; the launch traced here: 44.6 us
  Pallas kernels  43.3 us (97%)
  between operations  1.29 us (3%)
    pallas_call x1, Pallas kernels, on_device(): pl.pallas_call(kernel, out_shape=tuple((pltpu.VMEM(r.shape, r.dtype) for...  42.4 us

profile of v4, /device:TPU:1, one launch (start us, length us, event | category | flops | bytes accessed | tf_op | source)
XLA Modules:
  0.0 44.6 jit_solution(1010794447765224034)
XLA Ops:
  1.3 42.4 %shard_map.85 = (bf16[128,2048]{1,0:T(8,128)(2,1)S(1)}, f32[1,16,2048]{2,1,0:T(8,128)S(1)}, f32[1,16,256]{2,1,0:T(8,128)S(1)}) custom-call(bf16[128,2048]{1,0:T(8,128)(2,1)} %inputs_hbm.1, bf16[128,256]{1,0:T(8,128)(2,1)} %cot_hbm.1, bf16[8192,256]{1,0:T(8,128)(2,1)} %weight_hbm.1, bf16[1,16,2048]{2,1,0:T(8,128)(2,1)} %down_hbm.1, ...), custom_call_target="tpu_custom_call" | custom-call | tf_op jit(solution)/shard_map/pallas_call | solution.py:322
  43.7 0.9 %shard_map.86 = (bf16[128,2048]{1,0:T(8,128)(2,1)}, f32[1,16,2048]{2,1,0:T(8,128)}, f32[1,16,256]{2,1,0:T(8,128)}) custom-call(bf16[128,2048]{1,0:T(8,128)(2,1)S(1)} %get-tuple-element.6.out_vm, f32[1,16,2048]{2,1,0:T(8,128)S(1)} %get-tuple-element.7.grad_down_vm, f32[1,16,256]{2,1,0:T(8,128)S(1)} %get-tuple-element.8.grad_up_vm), custom_call_target="tpu_custom_call" | custom-call | tf_op jit(solution)/shard_map/pallas_call | solution.py:366

commit v5 on v4

--- a/solution.py
+++ b/solution.py
@@ -12,11 +12,16 @@
 
 Z, Y, CORES, X = 8, 4, 2, 4
 G = Z * CORES
+YC = Y * CORES
+HALF_G = G // 2
 ROWS, WIDTH, KEYS, RANK, LANES = 128, 2048, 256, 16, 128
-HALF, SPLIT = 64, 80
-
-STEPS = 14
-UP_ALL, ID_Y, DOWN_IN, ID_G, UP_PICK, DOWN_ALL, OUT_SUM, DOWN_PICK, TERM, IN_SUM, TERM_Y, UP_TERM, TERM_OWNER, UP_TERM_Y = range(STEPS)
+HALF, FIRST, SECOND = 64, 32, 64
+
+STEPS = 15
+(
+    UP_ALL, ID_Y, DOWN_IN, ID_G, UP_PICK, DOWN_ALL, OUT_SUM, DOWN_PICK, TERM, IN_SUM, TERM_FAR, TERM_NEAR, UP_TERM,
+    TERM_OWNER, UP_TERM_Y,
+) = range(STEPS)
 
 
 def dot(a, b, dims=((1,), (0,))):
@@ -41,6 +46,16 @@
         h = lax.rem(g + G // 2 + (1 - 2 * lax.rem(i, 2)) * lax.div(i + 1, 2), G)
         return h, (lax.div(h, CORES) * Y + y) * CORES + lax.rem(h, CORES)
 
+    def z_member(k):
+        h = lax.rem(z + k, Z)
+        return h, (h * Y + y) * CORES + c
+
+    p = y * CORES + c
+
+    def plane_member(k):
+        h = lax.rem(p + k, YC)
+        return h, z * YC + h
+
     def y_member(k):
         h = lax.rem(y + k, Y)
         return h, (z * Y + h) * CORES + c
@@ -62,8 +77,6 @@
             ((up_hbm, up_vm), (down_hbm, down_vm), (cot_hbm, cot_vm), (weight_hbm, weight), (inputs_hbm, xs))
         )
     ]
-    for load in loads:
-        load.start()
 
     barrier = pltpu.get_barrier_semaphore()
 
@@ -73,24 +86,20 @@
         pl.semaphore_signal(barrier, inc=1, device_id={"dp": device}, device_id_type=MESH)
 
     for k in (2, 1, 3):
-        pl.semaphore_signal(barrier, inc=1, device_id={"dp": y_member(k)[1]}, device_id_type=MESH)
+        device = y_member(k)[1]
+        pl.semaphore_signal(barrier, inc=1, device_id={"dp": device}, device_id_type=MESH)
+        pl.semaphore_signal(barrier, inc=1, device_id={"dp": device + 1 - 2 * c}, device_id_type=MESH)
         pl.semaphore_signal(barrier, inc=1, device_id={"tensor": lax.rem(mx + k, X)}, device_id_type=MESH)
 
+    for load in loads:
+        load.start()
     ids[0] = jnp.full((1, LANES), tenant_ref[0], jnp.int32).astype(F32)
     loads[0].wait()
     loads[1].wait()
     for q in range(G):
         down_in[q] = down_vm[0, :, q * LANES : (q + 1) * LANES]
-    pl.semaphore_wait(barrier, G - 1 + Y - 1 + X - 1)
-
-    @pl.loop(0, G - 1)
-    def _(i):
-        send(UP_ALL, up_vm.at[0], up_all.at[g], "dp", group_member(i)[1])
-
-    keep(UP_ALL, up_vm.at[0], up_all.at[g])
-    for k in (2, 1, 3):
-        send(ID_Y, ids.at[0], id_y.at[y], "dp", y_member(k)[1])
-    keep(ID_Y, ids.at[0], id_y.at[y])
+    pl.semaphore_wait(barrier, G - 1 + 2 * (Y - 1) + X - 1)
+
     my_rows = pl.ds(pl.multiple_of(g * RANK, RANK), RANK)
 
     @pl.loop(0, G - 1)
@@ -100,6 +109,13 @@
 
     keep(DOWN_IN, down_in.at[g], down_all.at[y, my_rows])
 
+    for k in (4, 3, 5, 2, 6, 1, 7):
+        send(UP_ALL, up_vm.at[0], up_all.at[z], "dp", z_member(k)[1])
+    keep(UP_ALL, up_vm.at[0], up_all.at[z])
+    for k in (4, 3, 5, 2, 6, 1, 7):
+        send(ID_Y, ids.at[0], id_y.at[p], "dp", plane_member(k)[1])
+    keep(ID_Y, ids.at[0], id_y.at[p])
+
     @pl.loop(0, G - 1)
     def _(i):
         send(ID_G, ids.at[0], id_g.at[g], "dp", group_member(i)[1])
@@ -112,20 +128,22 @@
         )
 
     low_half, high_half = pl.ds(0, HALF), pl.ds(HALF, ROWS - HALF)
-    first, rest = pl.ds(0, SPLIT), pl.ds(SPLIT, ROWS - SPLIT)
+    first, second = pl.ds(0, FIRST), pl.ds(FIRST, SECOND)
+    rest = pl.ds(FIRST + SECOND, ROWS - FIRST - SECOND)
     hops = (
         share(0, partial.at[1, low_half], hop.at[0], x_next),
         share(1, partial.at[1, high_half], hop.at[1], x_last),
     )
-    nearby = (
-        share(2, partial.at[0, first], arrived.at[0, first], x_next),
-        share(3, partial.at[2, first], arrived.at[2, first], x_last),
-    )
-    last = (
-        share(4, partial.at[0, rest], arrived.at[0, rest], x_next),
-        share(5, partial.at[2, rest], arrived.at[2, rest], x_last),
-        share(6, hop.at[0], arrived.at[1, low_half], x_next),
-        share(7, hop.at[1], arrived.at[1, high_half], x_last),
+    nearby = [
+        (
+            share(2 * i + 2, partial.at[0, part], arrived.at[0, part], x_next),
+            share(2 * i + 3, partial.at[2, part], arrived.at[2, part], x_last),
+        )
+        for i, part in enumerate((first, second, rest))
+    ]
+    relayed = (
+        share(8, hop.at[0], arrived.at[1, low_half], x_next),
+        share(9, hop.at[1], arrived.at[1, high_half], x_last),
     )
     loads[2].wait()
     cot = cot_vm[...]
@@ -140,27 +158,30 @@
         if k == 2:
             for copy in hops:
                 copy.start()
+        if k == 3:
+            for copy in nearby[0]:
+                copy.start()
 
     def place(t):
         t = t.astype(jnp.int32)
-        return (t >> 1) & 3, (t >> 3) * CORES + (t & 1)
+        return t >> 3, (t >> 1) & 3, t & 1
 
     rank = lax.broadcasted_iota(jnp.int32, (RANK, 1), 0)
-    slot = lax.broadcasted_iota(jnp.int32, (RANK, G * RANK), 1)
+    slot = lax.broadcasted_iota(jnp.int32, (RANK, Z * RANK), 1)
     received(ID_Y, id_y)
     wanted = []
-    for h in range(Y):
-        t_y, t_g = place(jnp.broadcast_to(id_y[h, :, :1], (RANK, 1)))
-        wanted.append((slot == jnp.where(t_y == y, t_g * RANK + rank, -1)).astype(F32).astype(BF16))
+    for h in range(YC):
+        t_z, t_y, t_c = place(jnp.broadcast_to(id_y[h, :, :1], (RANK, 1)))
+        wanted.append((slot == jnp.where(t_y * CORES + t_c == p, t_z * RANK + rank, -1)).astype(F32).astype(BF16))
     wanted = jnp.concatenate(wanted, axis=0)
     received(UP_ALL, up_all)
-    chosen = dot(wanted, up_all[...].reshape(G * RANK, KEYS)).astype(BF16)
-    for h in range(Y):
+    chosen = dot(wanted, up_all[...].reshape(Z * RANK, KEYS)).astype(BF16)
+    for h in range(YC):
         up_send[h] = chosen[h * RANK : (h + 1) * RANK]
-    for k in (2, 1, 3):
-        h, device = y_member(k)
-        send(UP_PICK, up_send.at[h], up_recv.at[y], "dp", device)
-    keep(UP_PICK, up_send.at[y], up_recv.at[y])
+    for k in (4, 3, 5, 2, 6, 1, 7):
+        h, device = plane_member(k)
+        send(UP_PICK, up_send.at[h], up_recv.at[p], "dp", device)
+    keep(UP_PICK, up_send.at[p], up_recv.at[p])
 
     received(DOWN_IN, down_all.at[y])
     for k in (2, 1, 3):
@@ -168,23 +189,28 @@
 
     received(ID_G, id_g)
     slot = lax.broadcasted_iota(jnp.int32, (RANK, Y * G * RANK), 1)
-    column = lax.broadcasted_iota(jnp.int32, (RANK, Y * RANK), 1)
+    for h in range(G):
+        t_z, t_y, t_c = place(jnp.broadcast_to(id_g[h, :, :1], (RANK, 1)))
+        t_slot = t_y * G + t_z * CORES + t_c
+        pick[h * RANK : (h + 1) * RANK, :] = (slot == t_slot * RANK + rank).astype(F32).astype(BF16)
+    slot = lax.broadcasted_iota(jnp.int32, (RANK, YC * RANK), 1)
     mine = []
-    for h in range(G):
-        t_y, t_g = place(jnp.broadcast_to(id_g[h, :, :1], (RANK, 1)))
-        pick[h * RANK : (h + 1) * RANK, :] = (slot == (t_y * G + t_g) * RANK + rank).astype(F32).astype(BF16)
-        mine.append((column == jnp.where(t_g == g, t_y * RANK + rank, -1)).astype(F32).astype(BF16))
+    for h in range(Z):
+        t_z, t_y, t_c = place(jnp.broadcast_to(id_g[h * CORES + c, :, :1], (RANK, 1)))
+        mine.append((slot == jnp.where(t_z == z, (t_y * CORES + t_c) * RANK + rank, -1)).astype(F32).astype(BF16))
     mine = jnp.concatenate(mine, axis=0)
 
     def pick_of(q):
         return pick[:, q * G * RANK : (q + 1) * G * RANK]
 
     received(UP_PICK, up_recv)
-    up_b = (up_recv[0].astype(F32) + up_recv[1].astype(F32)) + (up_recv[2].astype(F32) + up_recv[3].astype(F32))
+    up_b = up_recv[0].astype(F32)
+    for h in range(1, YC):
+        up_b += up_recv[h].astype(F32)
     out_sum[mx] = ADAPTER_SCALE * dot(up_b.astype(BF16), cot, ((1,), (1,)))
     for k in (2, 1, 3):
         send(OUT_SUM, out_sum.at[mx], out_sum.at[mx], "tensor", lax.rem(mx + k, X))
-    for copy in nearby:
+    for copy in nearby[1]:
         copy.start()
 
     received(DOWN_ALL, down_all.at[pl.ds(0, Y - 1)])
@@ -222,53 +248,57 @@
         send(IN_SUM, in_sum.at[mx], in_sum.at[mx], "tensor", lax.rem(mx + k, X))
     for copy in hops:
         copy.wait_recv()
-    for copy in last:
+    for copy in relayed + nearby[2]:
         copy.start()
     own[...] += dot(low_out, down_b, ((0,), (0,)))
 
     received(TERM, term_recv)
     terms = term_recv[...].reshape(G * RANK, LANES)
     for q in range(Y):
-        term_y_send[q] = dot(pick_of(q), terms, ((0,), (0,))).astype(BF16)
-    for k in (2, 1, 3):
-        h, device = y_member(k)
-        send(TERM_Y, term_y_send.at[h], term_y_recv.at[y], "dp", device)
-    keep(TERM_Y, term_y_send.at[y], term_y_recv.at[y])
+        sums = dot(pick_of(q), terms, ((0,), (0,))).astype(BF16)
+        for h in range(G):
+            term_y_send[q, lax.rem(h - g + G + G - 4, G)] = sums[h * RANK : (h + 1) * RANK]
+    halves = ((TERM_FAR, pl.ds(0, HALF_G)), (TERM_NEAR, pl.ds(HALF_G, HALF_G)))
+    for step, half in halves:
+        for k in (2, 1, 3):
+            h, device = y_member(k)
+            send(step, term_y_send.at[h, half], term_y_recv.at[y, half], "dp", device)
+        keep(step, term_y_send.at[y, half], term_y_recv.at[y, half])
 
     received(IN_SUM, in_sum.at[pl.ds(0, X - 1)])
     low_in = ((in_sum[0] + in_sum[1]) + (in_sum[2] + in_sum[3])).astype(BF16)
     up_term[...] = (ADAPTER_SCALE * dot(low_in, cot)).astype(BF16)
 
-    @pl.loop(0, G - 1)
-    def _(i):
-        send(UP_TERM, up_term, up_term_all.at[g], "dp", group_member(i)[1])
-
-    keep(UP_TERM, up_term, up_term_all.at[g])
-
-    received(TERM_Y, term_y_recv)
-    for h in range(G):
-        rows = slice(h * RANK, (h + 1) * RANK)
-        term_owner_send[h] = (term_y_recv[0, rows].astype(F32) + term_y_recv[1, rows].astype(F32)) + (
-            term_y_recv[2, rows].astype(F32) + term_y_recv[3, rows].astype(F32)
-        )
-
-    @pl.loop(0, G - 1)
-    def _(i):
-        h, device = group_member(i)
-        send(TERM_OWNER, term_owner_send.at[h], term_owner_recv.at[g], "dp", device)
-
-    keep(TERM_OWNER, term_owner_send.at[g], term_owner_recv.at[g])
+    for k in (4, 3, 5, 2, 6, 1, 7):
+        send(UP_TERM, up_term, up_term_all.at[z], "dp", z_member(k)[1])
+    keep(UP_TERM, up_term, up_term_all.at[z])
+
+    for step, half in halves:
+        received(step, term_y_recv.at[pl.ds(0, Y), half])
+        for j in range(half.start, half.start + HALF_G):
+            term_owner_send[j] = (term_y_recv[0, j].astype(F32) + term_y_recv[1, j].astype(F32)) + (
+                term_y_recv[2, j].astype(F32) + term_y_recv[3, j].astype(F32)
+            )
+        for j in (4, 3, 5, 2, 6, 1, 7, 0):
+            place_j = half.start + j
+            h = lax.rem(g + 4 + place_j, G)
+            if place_j == G - 4:
+                keep(TERM_OWNER, term_owner_send.at[place_j], term_owner_recv.at[g])
+            else:
+                device = (lax.div(h, CORES) * Y + y) * CORES + lax.rem(h, CORES)
+                send(TERM_OWNER, term_owner_send.at[place_j], term_owner_recv.at[g], "dp", device)
 
     received(UP_TERM, up_term_all)
-    sums = dot(mine, up_term_all[...].reshape(G * RANK, KEYS), ((0,), (0,)))
-    for h in range(Y):
+    sums = dot(mine, up_term_all[...].reshape(Z * RANK, KEYS), ((0,), (0,)))
+    for h in range(YC):
         up_term_y_send[h] = sums[h * RANK : (h + 1) * RANK]
-    for k in (2, 1, 3):
-        h, device = y_member(k)
-        send(UP_TERM_Y, up_term_y_send.at[h], up_term_y_recv.at[y], "dp", device)
-    keep(UP_TERM_Y, up_term_y_send.at[y], up_term_y_recv.at[y])
-
-    for copy in nearby + last:
+    for k in (4, 3, 5, 2, 6, 1, 7):
+        h, device = plane_member(k)
+        send(UP_TERM_Y, up_term_y_send.at[h], up_term_y_recv.at[p], "dp", device)
+    keep(UP_TERM_Y, up_term_y_send.at[p], up_term_y_recv.at[p])
+
+    shares = nearby[0] + nearby[1] + nearby[2] + relayed
+    for copy in shares:
         copy.wait_recv()
     for i in range(WIDTH // KEYS):
         columns = slice(i * KEYS, (i + 1) * KEYS)
@@ -280,18 +310,23 @@
     for h in range(G):
         grad_down_ref[0, :, h * LANES : (h + 1) * LANES] = term_owner_recv[h]
     received(UP_TERM_Y, up_term_y_recv)
-    grad_up_ref[0] = (up_term_y_recv[0] + up_term_y_recv[1]) + (up_term_y_recv[2] + up_term_y_recv[3])
-
-    for copy in hops + nearby + last:
+    total = up_term_y_recv[0]
+    for h in range(1, YC):
+        total += up_term_y_recv[h]
+    grad_up_ref[0] = total
+
+    for copy in hops + shares:
         copy.wait_send()
     for step, sent, peers in (
-        (UP_ALL, up_all, G - 1), (ID_Y, id_y, Y - 1), (DOWN_IN, down_in, G - 1), (ID_G, id_g, G - 1),
-        (UP_PICK, up_send, Y - 1), (DOWN_ALL, down_all, Y - 1), (OUT_SUM, out_sum, X - 1),
+        (UP_ALL, up_all, Z - 1), (ID_Y, id_y, YC - 1), (DOWN_IN, down_in, G - 1), (ID_G, id_g, G - 1),
+        (UP_PICK, up_send, YC - 1), (DOWN_ALL, down_all, Y - 1), (OUT_SUM, out_sum, X - 1),
         (DOWN_PICK, down_send, G - 1), (TERM, term_send, G - 1), (IN_SUM, in_sum, X - 1),
-        (TERM_Y, term_y_send, Y - 1), (UP_TERM, up_term_all, G - 1), (TERM_OWNER, term_owner_send, G - 1),
-        (UP_TERM_Y, up_term_y_send, Y - 1),
+        (UP_TERM, up_term_all, Z - 1), (TERM_OWNER, term_owner_send, G - 1), (UP_TERM_Y, up_term_y_send, YC - 1),
     ):
         view = sent.at[pl.ds(0, peers)]
+        pltpu.make_async_copy(view, view, send_sem.at[step]).wait()
+    for step, half in halves:
+        view = term_y_send.at[pl.ds(0, Y - 1), half]
         pltpu.make_async_copy(view, view, send_sem.at[step]).wait()
 
 
@@ -336,28 +371,28 @@
             pltpu.VMEM((2, HALF, WIDTH), BF16),
             pltpu.VMEM((1, 1, LANES), F32),
             pltpu.VMEM((G * RANK, Y * G * RANK), BF16),
-            pltpu.VMEM((G, RANK, KEYS), BF16),
-            pltpu.VMEM((Y, 1, LANES), F32),
+            pltpu.VMEM((Z, RANK, KEYS), BF16),
+            pltpu.VMEM((YC, 1, LANES), F32),
             pltpu.VMEM((G, RANK, LANES), BF16),
             pltpu.VMEM((Y, G * RANK, LANES), BF16),
             pltpu.VMEM((G, 1, LANES), F32),
-            pltpu.VMEM((Y, RANK, KEYS), BF16),
-            pltpu.VMEM((Y, RANK, KEYS), BF16),
+            pltpu.VMEM((YC, RANK, KEYS), BF16),
+            pltpu.VMEM((YC, RANK, KEYS), BF16),
             pltpu.VMEM((X, RANK, ROWS), F32),
             pltpu.VMEM((G, RANK, LANES), BF16),
             pltpu.VMEM((G, RANK, LANES), BF16),
             pltpu.VMEM((X, RANK, ROWS), F32),
             pltpu.VMEM((G, RANK, LANES), BF16),
             pltpu.VMEM((G, RANK, LANES), BF16),
-            pltpu.VMEM((Y, G * RANK, LANES), BF16),
-            pltpu.VMEM((Y, G * RANK, LANES), BF16),
+            pltpu.VMEM((Y, G, RANK, LANES), BF16),
+            pltpu.VMEM((Y, G, RANK, LANES), BF16),
             pltpu.VMEM((G, RANK, LANES), F32),
             pltpu.VMEM((G, RANK, LANES), F32),
             pltpu.VMEM((RANK, KEYS), BF16),
-            pltpu.VMEM((G, RANK, KEYS), BF16),
-            pltpu.VMEM((Y, RANK, KEYS), F32),
-            pltpu.VMEM((Y, RANK, KEYS), F32),
-            dma((5,)), dma((STEPS,)), dma((STEPS,)), dma((8,)), dma((8,)),
+            pltpu.VMEM((Z, RANK, KEYS), BF16),
+            pltpu.VMEM((YC, RANK, KEYS), F32),
+            pltpu.VMEM((YC, RANK, KEYS), F32),
+            dma((5,)), dma((STEPS,)), dma((STEPS,)), dma((10,)), dma((10,)),
         ],
         compiler_params=pltpu.CompilerParams(
             collective_id=0, has_side_effects=True, vmem_limit_bytes=60 << 20

time: 44.7 us -> 42.2 us (0.944)
  Pallas kernels: 43.3 us -> 40.8 us
    pallas_call x1, Pallas kernels: 42.4 us -> 39.9 us  [on_device(): pl.pallas_call(kernel, out_shape=tuple((pltpu.VMEM(r.shape, r.dtype) for...]
where the time goes in v5:
time: 42.2 us; the launch traced here: 42.1 us
  Pallas kernels  40.8 us (97%)
  between operations  1.29 us (3%)
    pallas_call x1, Pallas kernels, on_device(): pl.pallas_call(kernel, out_shape=tuple((pltpu.VMEM(r.shape, r.dtype) for...  39.9 us
    pallas_call x1, Pallas kernels, on_device(): pl.pallas_call(store_kernel, out_shape=results, in_specs=[anywhere] * 3,...  0.86 us

profile of v5, /device:TPU:1, one launch (start us, length us, event | category | flops | bytes accessed | tf_op | source)
XLA Modules:
  0.0 42.1 jit_solution(6060079600596576635)
XLA Ops:
  1.3 39.9 %shard_map.85 = (bf16[128,2048]{1,0:T(8,128)(2,1)S(1)}, f32[1,16,2048]{2,1,0:T(8,128)S(1)}, f32[1,16,256]{2,1,0:T(8,128)S(1)}) custom-call(bf16[128,2048]{1,0:T(8,128)(2,1)} %inputs_hbm.1, bf16[128,256]{1,0:T(8,128)(2,1)} %cot_hbm.1, bf16[8192,256]{1,0:T(8,128)(2,1)} %weight_hbm.1, bf16[1,16,2048]{2,1,0:T(8,128)(2,1)} %down_hbm.1, ...), custom_call_target="tpu_custom_call" | custom-call | tf_op jit(solution)/shard_map/pallas_call | solution.py:357
  41.2 0.9 %shard_map.86 = (bf16[128,2048]{1,0:T(8,128)(2,1)}, f32[1,16,2048]{2,1,0:T(8,128)}, f32[1,16,256]{2,1,0:T(8,128)}) custom-call(bf16[128,2048]{1,0:T(8,128)(2,1)S(1)} %get-tuple-element.6.out_vm, f32[1,16,2048]{2,1,0:T(8,128)S(1)} %get-tuple-element.7.grad_down_vm, f32[1,16,256]{2,1,0:T(8,128)S(1)} %get-tuple-element.8.grad_up_vm), custom_call_target="tpu_custom_call" | custom-call | tf_op jit(solution)/shard_map/pallas_call | solution.py:401

commit v6 on v5

--- a/solution.py
+++ b/solution.py
@@ -193,11 +193,11 @@
         t_z, t_y, t_c = place(jnp.broadcast_to(id_g[h, :, :1], (RANK, 1)))
         t_slot = t_y * G + t_z * CORES + t_c
         pick[h * RANK : (h + 1) * RANK, :] = (slot == t_slot * RANK + rank).astype(F32).astype(BF16)
-    slot = lax.broadcasted_iota(jnp.int32, (RANK, YC * RANK), 1)
+    slot = lax.broadcasted_iota(jnp.int32, (RANK, Y * RANK), 1)
     mine = []
-    for h in range(Z):
-        t_z, t_y, t_c = place(jnp.broadcast_to(id_g[h * CORES + c, :, :1], (RANK, 1)))
-        mine.append((slot == jnp.where(t_z == z, (t_y * CORES + t_c) * RANK + rank, -1)).astype(F32).astype(BF16))
+    for h in range(G):
+        t_z, t_y, t_c = place(jnp.broadcast_to(id_g[h, :, :1], (RANK, 1)))
+        mine.append((slot == jnp.where(t_z * CORES + t_c == g, t_y * RANK + rank, -1)).astype(F32).astype(BF16))
     mine = jnp.concatenate(mine, axis=0)
 
     def pick_of(q):
@@ -269,9 +269,11 @@
     low_in = ((in_sum[0] + in_sum[1]) + (in_sum[2] + in_sum[3])).astype(BF16)
     up_term[...] = (ADAPTER_SCALE * dot(low_in, cot)).astype(BF16)
 
-    for k in (4, 3, 5, 2, 6, 1, 7):
-        send(UP_TERM, up_term, up_term_all.at[z], "dp", z_member(k)[1])
-    keep(UP_TERM, up_term, up_term_all.at[z])
+    @pl.loop(0, G - 1)
+    def _(i):
+        send(UP_TERM, up_term, up_term_all.at[g], "dp", group_member(i)[1])
+
+    keep(UP_TERM, up_term, up_term_all.at[g])
 
     for step, half in halves:
         received(step, term_y_recv.at[pl.ds(0, Y), half])
@@ -289,13 +291,13 @@
                 send(TERM_OWNER, term_owner_send.at[place_j], term_owner_recv.at[g], "dp", device)
 
     received(UP_TERM, up_term_all)
-    sums = dot(mine, up_term_all[...].reshape(Z * RANK, KEYS), ((0,), (0,)))
-    for h in range(YC):
+    sums = dot(mine, up_term_all[...].reshape(G * RANK, KEYS), ((0,), (0,)))
+    for h in range(Y):
         up_term_y_send[h] = sums[h * RANK : (h + 1) * RANK]
-    for k in (4, 3, 5, 2, 6, 1, 7):
-        h, device = plane_member(k)
-        send(UP_TERM_Y, up_term_y_send.at[h], up_term_y_recv.at[p], "dp", device)
-    keep(UP_TERM_Y, up_term_y_send.at[p], up_term_y_recv.at[p])
+    for k in (2, 1, 3):
+        h, device = y_member(k)
+        send(UP_TERM_Y, up_term_y_send.at[h], up_term_y_recv.at[y], "dp", device)
+    keep(UP_TERM_Y, up_term_y_send.at[y], up_term_y_recv.at[y])
 
     shares = nearby[0] + nearby[1] + nearby[2] + relayed
     for copy in shares:
@@ -310,10 +312,7 @@
     for h in range(G):
         grad_down_ref[0, :, h * LANES : (h + 1) * LANES] = term_owner_recv[h]
     received(UP_TERM_Y, up_term_y_recv)
-    total = up_term_y_recv[0]
-    for h in range(1, YC):
-        total += up_term_y_recv[h]
-    grad_up_ref[0] = total
+    grad_up_ref[0] = (up_term_y_recv[0] + up_term_y_recv[1]) + (up_term_y_recv[2] + up_term_y_recv[3])
 
     for copy in hops + shares:
         copy.wait_send()
@@ -321,7 +320,7 @@
         (UP_ALL, up_all, Z - 1), (ID_Y, id_y, YC - 1), (DOWN_IN, down_in, G - 1), (ID_G, id_g, G - 1),
         (UP_PICK, up_send, YC - 1), (DOWN_ALL, down_all, Y - 1), (OUT_SUM, out_sum, X - 1),
         (DOWN_PICK, down_send, G - 1), (TERM, term_send, G - 1), (IN_SUM, in_sum, X - 1),
-        (UP_TERM, up_term_all, Z - 1), (TERM_OWNER, term_owner_send, G - 1), (UP_TERM_Y, up_term_y_send, YC - 1),
+        (UP_TERM, up_term_all, G - 1), (TERM_OWNER, term_owner_send, G - 1), (UP_TERM_Y, up_term_y_send, Y - 1),
     ):
         view = sent.at[pl.ds(0, peers)]
         pltpu.make_async_copy(view, view, send_sem.at[step]).wait()
@@ -389,9 +388,9 @@
             pltpu.VMEM((G, RANK, LANES), F32),
             pltpu.VMEM((G, RANK, LANES), F32),
             pltpu.VMEM((RANK, KEYS), BF16),
-            pltpu.VMEM((Z, RANK, KEYS), BF16),
-            pltpu.VMEM((YC, RANK, KEYS), F32),
-            pltpu.VMEM((YC, RANK, KEYS), F32),
+            pltpu.VMEM((G, RANK, KEYS), BF16),
+            pltpu.VMEM((Y, RANK, KEYS), F32),
+            pltpu.VMEM((Y, RANK, KEYS), F32),
             dma((5,)), dma((STEPS,)), dma((STEPS,)), dma((10,)), dma((10,)),
         ],
         compiler_params=pltpu.CompilerParams(

time: 42.2 us -> 42.2 us (level)
  no operation moved by 1% of the time
where the time goes in v6:
time: 42.2 us; the launch traced here: 42 us
  Pallas kernels  40.7 us (96%)
  between operations  1.29 us (3%)
    pallas_call x1, Pallas kernels, on_device(): pl.pallas_call(kernel, out_shape=tuple((pltpu.VMEM(r.shape, r.dtype) for...  39.9 us
    pallas_call x1, Pallas kernels, on_device(): pl.pallas_call(store_kernel, out_shape=results, in_specs=[anywhere] * 3,...  0.86 us

profile of v6, /device:TPU:1, one launch (start us, length us, event | category | flops | bytes accessed | tf_op | source)
XLA Modules:
  0.0 42.0 jit_solution(8111119694830056853)
XLA Ops:
  1.3 39.9 %shard_map.85 = (bf16[128,2048]{1,0:T(8,128)(2,1)S(1)}, f32[1,16,2048]{2,1,0:T(8,128)S(1)}, f32[1,16,256]{2,1,0:T(8,128)S(1)}) custom-call(bf16[128,2048]{1,0:T(8,128)(2,1)} %inputs_hbm.1, bf16[128,256]{1,0:T(8,128)(2,1)} %cot_hbm.1, bf16[8192,256]{1,0:T(8,128)(2,1)} %weight_hbm.1, bf16[1,16,2048]{2,1,0:T(8,128)(2,1)} %down_hbm.1, ...), custom_call_target="tpu_custom_call" | custom-call | tf_op jit(solution)/shard_map/pallas_call | solution.py:356
  41.2 0.9 %shard_map.86 = (bf16[128,2048]{1,0:T(8,128)(2,1)}, f32[1,16,2048]{2,1,0:T(8,128)}, f32[1,16,256]{2,1,0:T(8,128)}) custom-call(bf16[128,2048]{1,0:T(8,128)(2,1)S(1)} %get-tuple-element.6.out_vm, f32[1,16,2048]{2,1,0:T(8,128)S(1)} %get-tuple-element.7.grad_down_vm, f32[1,16,256]{2,1,0:T(8,128)S(1)} %get-tuple-element.8.grad_up_vm), custom_call_target="tpu_custom_call" | custom-call | tf_op jit(solution)/shard_map/pallas_call | solution.py:400
